TPU v7x, 512 devices: a whole 4x4x16 slice. The times are simulated.
512 devices in a mesh: mem: 4 (over x), gx: 16 (over z_lo, core), gy: 8 (over y, z_hi).
Axes of the slice: x: 4, y: 4, z: 16 (z_hi: 2, z_lo: 8; z = z_hi * 8 + z_lo), core: 2. Of those that a mesh axis runs over, the one named last changes fastest.
Arguments:
- members: bfloat16 [8, 64, 256, 1024], P('mem', None, 'gx', 'gy'), may hold values from -6 to 6
- gradient: float32 [64, 256, 1024], P(None, 'gx', 'gy'), may hold values from -6 to 6
- control: bfloat16 [8, 64, 256, 1024], P('mem', None, 'gx', 'gy'), may hold values from -6 to 6
- filter_rates: float32 [64], replicated, may hold values from 0.0009765625 to 0.03
- vertical_weights: float32 [64, 64], replicated, may hold values from -0.75 to 0.75
- band_widths: int32 [64], replicated, may hold values from 0 to 63, each once
Outputs:
- control_gradient: float32 [8, 64, 256, 1024], P('mem', None, 'gx', 'gy')
Inputs may be any that keep to these rules, and one draw needn't show every extreme that they name: `band_widths`: each of the values 0 to 63 appears once.
All inputs are finite; a program needn't handle non-finite values.
Results may differ from a plain program's by a relative error of at most 0.0003.
Values sent between devices are 32-bit elements; how exact they have to be, the bound alone decides.
A program may use at most 64 MiB of HBM per device.

v0:
```python
import functools

import jax
import jax.numpy as jnp
from jax import lax
from jax.experimental import pallas as pl
from jax.experimental.pallas import tpu as pltpu
from jax.sharding import PartitionSpec as P

MESH = pl.DeviceIdType.MESH
F32 = jnp.float32
BF16 = jnp.bfloat16

LEV, MEMBERS, NX, NY = 64, 8, 256, 1024
MEM, GX, GY = 4, 16, 8
KLOC = MEMBERS // MEM
BX, BY = NX // GX, NY // GY
ROWS = LEV * BX
GROUPS = LEV // 4
QUARTER = ROWS // MEM
CHUNKS = 4
CHUNK = LEV // CHUNKS

NT = (((1,), (1,)), ((), ()))
NN = (((1,), (0,)), ((), ()))
TN = (((0,), (0,)), ((), ()))


def dot(a, b, dims):
    return lax.dot_general(a, b, dims, preferred_element_type=F32)


def split(x):
    hi = x.astype(BF16)
    return hi, (x - hi.astype(F32)).astype(BF16)


def iota(shape, axis):
    return lax.broadcasted_iota(jnp.int32, shape, axis)


class Line:
    def __init__(self, rate, total, size, index):
        r = rate
        self.rate = r
        self.log = -r * (1.0 + r * (0.5 + r * (1.0 / 3 + r * (0.25 + r * (0.2 + r * (1.0 / 6))))))
        self.a = 1.0 - r
        self.g = self.a * self.a / (r * (1.0 + self.a))
        self.s = (index * size).astype(F32)
        self.last = self.s + (size - 1.0)
        self.n2 = 2.0 * total - self.last
        self.p_s = self.power(self.s)
        self.p_inv = self.power(-self.last)
        self.p_n2 = self.power(self.n2)
        self.ga = self.g * self.power(2.0 * total)
        self.G = 1.0 + 2.0 * self.g + self.ga
        self.total = total
        self.e = self.s + size

    def power(self, m):
        return jnp.exp(self.log * m)

    def sums(self, r1, r2, q1, q2):
        sa = self.p_inv * r1
        fq = self.p_s * q1
        sb = self.p_inv * (self.last * r1 - r2) + self.g * fq
        lh = fq - self.p_n2 * r1
        la = self.p_s * ((self.s + self.G) * q1 + q2) - self.p_n2 * ((self.n2 + self.G) * r1 + r2)
        return sa, sb, la, lh


def kernel(rates, rates_v, bands, weights, members, gradient, control, out,
           mem_v, grad_v, ctl_v, out_v, psum, total, rs_rcv, vbuf, zbuf, wtab, lsub, thi, tlo,
           mu, ysnd, yrcv, zsnd, zrcv, kap, xst, xpair, xin, xout, xss, xsr, fbuf,
           in_sem, rs_s, rs_r, ag_s, ag_r, y_s, y_r, h_s, h_r, p_s, p_r, c_s, c_r, d_s, d_r):
    i = lax.axis_index("mem")
    gx = lax.axis_index("gx")
    gy = lax.axis_index("gy")
    z, core = gx // 2, gx % 2
    yy, hh = gy // 2, gy % 2

    loads = [
        pltpu.make_async_copy(members, mem_v, in_sem.at[0]),
        pltpu.make_async_copy(gradient, grad_v, in_sem.at[1]),
        pltpu.make_async_copy(control, ctl_v, in_sem.at[2]),
    ]
    for load in loads:
        load.start()

    def signal(dev):
        pl.semaphore_signal(barrier, inc=1, device_id=dev, device_id_type=MESH)

    barrier = pltpu.get_barrier_semaphore()
    sibling = (i, gx + 1 - 2 * core, gy)
    across = (i, gx, gy + 1 - 2 * hh)
    peers = [((i + d) % MEM, gx, gy) for d in range(1, MEM)]
    y_at = [(yy + d) % 4 for d in range(1, 4)]
    signal(across)
    for d in range(3):
        signal(peers[d])
        signal((i, gx, y_at[d] * 2 + hh))
    signal(sibling)

    @pl.when(z > 0)
    def _():
        signal((i, gx - 2, gy))

    @pl.when(z < 7)
    def _():
        signal((i, gx + 2, gy))

    sub8 = iota((8, 128), 0)
    for t in range(LEV // 8):
        v = jnp.zeros((8, 128), F32)
        for j in range(8):
            v = jnp.where(sub8 == j, rates[t * 8 + j], v)
        lsub[t * 8:(t + 1) * 8, :] = v
    lane_lv = (iota((GROUPS, 128), 1) // BX) % 4
    row_g = iota((GROUPS, 128), 0)
    lev_id = row_g * 4 + lane_lv
    rate_lane = jnp.zeros((GROUPS, 128), F32)
    for l in range(LEV):
        rate_lane = jnp.where(lev_id == l, rates[l], rate_lane)
    ly = Line(rate_lane, NY, BY, gy)
    lx_rate = lsub[...]

    cell = iota((8, 128), 1).astype(F32)
    dist = jnp.where(sub8 < 2, 127.0 - cell, cell)
    factor = jnp.where((sub8 == 0) | (sub8 == 2), 1.0, jnp.where((sub8 == 1) | (sub8 == 3), dist, 0.0))

    def logs(r):
        return -r * (1.0 + r * (0.5 + r * (1.0 / 3 + r * (0.25 + r * (0.2 + r * (1.0 / 6))))))

    def basis(l, carry):
        lg = logs(jnp.broadcast_to(lsub[pl.ds(l, 1), :], (8, 128)))
        wtab[pl.ds(pl.multiple_of(l * 8, 8), 8), :] = jnp.exp(dist * lg) * factor
        return carry

    lax.fori_loop(0, LEV, basis, 0, unroll=4)

    loads[0].wait()
    for q in range(MEM):
        lo = q * QUARTER
        psum[lo:lo + QUARTER, :] = (mem_v[0, lo:lo + QUARTER, :].astype(F32)
                                    + mem_v[1, lo:lo + QUARTER, :].astype(F32))

    pl.semaphore_wait(barrier, 8 + (z > 0).astype(jnp.int32) + (z < 7).astype(jnp.int32))

    rs = []
    for d in range(3):
        at = pl.multiple_of(peers[d][0] * QUARTER, QUARTER)
        cp = pltpu.make_async_remote_copy(
            src_ref=psum.at[pl.ds(at, QUARTER)], dst_ref=rs_rcv.at[d],
            send_sem=rs_s.at[d], recv_sem=rs_r.at[d], device_id=peers[d], device_id_type=MESH)
        cp.start()
        rs.append(cp)

    di = jnp.abs(iota((BY, BY), 0) - iota((BY, BY), 1)).astype(F32)

    def toeplitz(l, carry):
        r = jnp.broadcast_to(lsub[pl.ds(l, 1), :], (8, 128))
        lg = logs(r)
        a = 1.0 - r
        c = 1.0 + 2.0 * (a * a / (r * (1.0 + a)))
        lg = jnp.broadcast_to(lg[0:1, :], (BY, BY))
        c = jnp.broadcast_to(c[0:1, :], (BY, BY))
        t = jnp.exp(di * lg) * (di + c)
        hi, lo = split(t)
        at = pl.multiple_of(l * BY, BY)
        thi[pl.ds(at, BY), :] = hi
        tlo[pl.ds(at, BY), :] = lo
        return carry

    lax.fori_loop(0, LEV, toeplitz, 0)

    own = pl.multiple_of(i * QUARTER, QUARTER)
    for cp in rs:
        cp.wait()
    total[pl.ds(own, QUARTER), :] = (psum[pl.ds(own, QUARTER), :] + rs_rcv[0] + rs_rcv[1] + rs_rcv[2])
    ag = []
    for d in range(3):
        cp = pltpu.make_async_remote_copy(
            src_ref=total.at[pl.ds(own, QUARTER)], dst_ref=total.at[pl.ds(own, QUARTER)],
            send_sem=ag_s.at[d], recv_sem=ag_r.at[d], device_id=peers[d], device_id_type=MESH)
        cp.start()
        ag.append(cp)
    loads[1].wait()
    for cp in ag:
        cp.wait()

    def product(g, carry):
        at = pl.multiple_of(g * 64, 64)
        mean = total[pl.ds(at, 64), :] * (1.0 / MEMBERS)
        gr = grad_v[pl.ds(at, 64), :]
        v0 = (mem_v[0, pl.ds(at, 64), :].astype(F32) - mean) * gr
        v1 = (mem_v[1, pl.ds(at, 64), :].astype(F32) - mean) * gr
        vbuf[0, pl.ds(at, 64), :] = v0
        vbuf[1, pl.ds(at, 64), :] = v1
        vh, vl = split(jnp.concatenate([v0, v1], axis=0))
        wh, wl = split(wtab[pl.ds(pl.multiple_of(g * 32, 32), 32), :])
        res = dot(wh, vh, NT) + dot(wh, vl, NT) + dot(wl, vh, NT)
        lane = (iota((8, 128), 1) // BX) % 4
        m8 = jnp.zeros((8, 128), F32)
        for lv in range(4):
            m8 = jnp.where(lane == lv, res[lv * 8:lv * 8 + 8, :], m8)
        mu[pl.ds(pl.multiple_of(g * 8, 8), 8), :] = m8
        return carry

    lax.fori_loop(0, GROUPS, product, 0)

    r1, r2, q1, q2 = [mu[pl.ds(q, GROUPS, stride=8), :] for q in range(4)]
    own_y = ly.sums(r1, r2, q1, q2)
    for q in range(4):
        ysnd[q] = own_y[q]
    ycp = []
    for d in range(3):
        part = pl.multiple_of(jnp.where(y_at[d] > yy, 0, 2), 2)
        cp = pltpu.make_async_remote_copy(
            src_ref=ysnd.at[pl.ds(part, 2)], dst_ref=yrcv.at[d],
            send_sem=y_s.at[d], recv_sem=y_r.at[d], device_id=(i, gx, y_at[d] * 2 + hh), device_id_type=MESH)
        cp.start()
        ycp.append(cp)

    def local_y(l, carry):
        at = pl.multiple_of(l * BX, BX)
        tt = pl.multiple_of(l * BY, BY)
        v = jnp.concatenate([vbuf[0, pl.ds(at, BX), :], vbuf[1, pl.ds(at, BX), :]], axis=0)
        vh, vl = split(v)
        th = thi[pl.ds(tt, BY), :]
        res = dot(vh, th, NN) + dot(vl, th, NN) + dot(vh, tlo[pl.ds(tt, BY), :], NN)
        zbuf[0, pl.ds(at, BX), :] = res[0:BX]
        zbuf[1, pl.ds(at, BX), :] = res[BX:]
        return carry

    lax.fori_loop(0, LEV // 2, local_y, 0)

    for cp in ycp:
        cp.wait()
    zero = jnp.zeros((GROUPS, 128), F32)
    sa = sb = la = lh = zero
    for d in range(3):
        from_left = (yy - (d + 1)) >= 0
        u, w = yrcv[d, 0], yrcv[d, 1]
        sa = sa + jnp.where(from_left, u, 0.0)
        sb = sb + jnp.where(from_left, w, 0.0)
        la = la + jnp.where(from_left, 0.0, u)
        lh = lh + jnp.where(from_left, 0.0, w)
    zsnd[0] = sa + jnp.where(hh == 0, own_y[0], 0.0)
    zsnd[1] = sb + jnp.where(hh == 0, own_y[1], 0.0)
    zsnd[2] = la + jnp.where(hh == 1, own_y[2], 0.0)
    zsnd[3] = lh + jnp.where(hh == 1, own_y[3], 0.0)
    hcp = pltpu.make_async_remote_copy(
        src_ref=zsnd, dst_ref=zrcv, send_sem=h_s, recv_sem=h_r, device_id=across, device_id_type=MESH)
    hcp.start()
    lax.fori_loop(LEV // 2, LEV, local_y, 0)
    lx = Line(lx_rate, NX, BX, gx)
    hcp.wait()
    sa = sa + zrcv[0]
    sb = sb + zrcv[1]
    la = la + zrcv[2]
    lh = lh + zrcv[3]
    k1 = (ly.p_n2 * (sb - sa * (ly.n2 + ly.G)) + ly.p_inv * (la - lh * ly.last)
          + ly.ga * ly.p_inv * (ly.p_s * q1)
          - ly.p_n2 * ly.p_inv * ((2.0 * (NY - ly.last) + ly.G) * r1 + r2))
    k2 = lh * ly.p_inv - sa * ly.p_n2 - ly.p_n2 * ly.p_inv * r1
    k3 = ly.p_s * (sa * (ly.s + ly.G) - sb - lh * ly.g + ly.ga * ly.p_inv * r1 - ly.g * ly.p_s * q1)
    k4 = sa * ly.p_s
    for q, k in enumerate((k1, k2, k3, k4, zero, zero, zero, zero)):
        kap[pl.ds(q, GROUPS, stride=8), :] = k

    def synth(g, carry):
        at = pl.multiple_of(g * 64, 64)
        k8 = kap[pl.ds(pl.multiple_of(g * 8, 8), 8), :]
        lane = (iota((8, 128), 1) // BX) % 4
        big = jnp.concatenate([jnp.where(lane == lv, k8, 0.0) for lv in range(4)], axis=0)
        kh, kl = split(big.T)
        wh, wl = split(wtab[pl.ds(pl.multiple_of(g * 32, 32), 32), :])
        res = dot(kh, wh, NN) + dot(kl, wh, NN) + dot(kh, wl, NN)
        zbuf[0, pl.ds(at, 64), :] += res[0:64]
        zbuf[1, pl.ds(at, 64), :] += res[64:]
        return carry

    lax.fori_loop(0, GROUPS, synth, 0)

    a_sub = lx.a

    def x_moments(k):
        r1 = jnp.zeros((LEV, 128), F32)
        r2, q1, q2 = r1, r1, r1
        for x in range(BX):
            v = zbuf[k, pl.ds(x, LEV, stride=BX), :]
            t = a_sub * r1
            r2 = a_sub * r2 + t
            r1 = t + v
            v = zbuf[k, pl.ds(BX - 1 - x, LEV, stride=BX), :]
            t = a_sub * q1
            q2 = a_sub * q2 + t
            q1 = t + v
        return lx.sums(r1, r2, q1, q2)

    for k in range(KLOC):
        for q, s in enumerate(x_moments(k)):
            xst[k, q] = s
    pcp = pltpu.make_async_remote_copy(
        src_ref=xst.at[1 - core], dst_ref=xpair, send_sem=p_s, recv_sem=p_r, device_id=sibling, device_id_type=MESH)
    pcp.start()
    pcp.wait()

    def chain(turn):
        way = ((z >= 4).astype(jnp.int32) + turn) % 2
        has_in = jnp.where(way == 0, z > 0, z < 7)
        has_out = jnp.where(way == 0, z < 7, z > 0)
        target = (i, gx + 2 - 4 * way, gy)
        part = pl.multiple_of(way * 2, 2)

        def copy(c):
            rows = pl.ds(c * CHUNK, CHUNK)
            return pltpu.make_async_remote_copy(
                src_ref=xout.at[way, :, rows], dst_ref=xin.at[way, :, rows],
                send_sem=c_s.at[way, c], recv_sem=c_r.at[way, c], device_id=target, device_id_type=MESH)

        @pl.when(jnp.logical_not(has_in))
        def _():
            xin[way] = jnp.zeros((2, LEV, 128), F32)

        for c in range(CHUNKS):
            rows = slice(c * CHUNK, (c + 1) * CHUNK)

            @pl.when(has_in)
            def _():
                copy(c).wait_recv()

            @pl.when(has_out)
            def _():
                xout[way, :, rows] = (xin[way, :, rows] + xst[core, pl.ds(part, 2), rows]
                                      + xpair[pl.ds(part, 2), rows])
                copy(c).start()

        add = jnp.where(way == core, 1.0, 0.0)
        xss[way] = xin[way] + add * xst[core, pl.ds(part, 2)]
        sib = pltpu.make_async_remote_copy(
            src_ref=xss.at[way], dst_ref=xsr.at[way], send_sem=d_s.at[way], recv_sem=d_r.at[way],
            device_id=sibling, device_id_type=MESH)
        sib.start()
        xin[way] = xin[way] + (1.0 - add) * xpair[pl.ds(part, 2)]
        return way, has_out, copy, sib

    done = [chain(0), chain(1)]
    for way, has_out, copy, sib in done:
        for c in range(CHUNKS):
            @pl.when(has_out)
            def _():
                copy(c).wait_send()
    for way, has_out, copy, sib in done:
        sib.wait()

    g, ga, s, e, G = lx.g, lx.ga, lx.s, lx.e, lx.G
    ge = 1.0 + g
    p_e, p_me, p_2e = lx.power(e), lx.power(-e), lx.power(2.0 * NX - e)
    hx = p_e - p_2e
    ux = p_e * (e + G) - p_2e * (2.0 * NX - e + G)
    p_s1, p_ms1 = lx.power(s - 1.0), lx.power(-s - 1.0)
    c2a = s + g + ga - g * lx.power(2.0 * NX - 2.0 * s)
    c2h = g * (p_ms1 - p_s1)
    mine = core == 0

    for k in range(KLOC):
        local = core == k
        sa = jnp.where(local, xin[0, 0], xsr[0, 0])
        sb = jnp.where(local, xin[0, 1], xsr[0, 1])
        la = jnp.where(local, xin[1, 0], xsr[1, 0])
        lh = jnp.where(local, xin[1, 1], xsr[1, 1])
        oa, ob, _, oh = xst[k, 0], xst[k, 1], xst[k, 2], xst[k, 3]
        c1 = p_s1 * sa
        d1 = ge * (hx * (sa + oa) + p_me * lh)
        c2 = ge * (p_s1 * (c2a * sa - sb) + c2h * (oh + lh))
        d2 = ge * ge * (ux * (sa + oa) - hx * (sb + ob) + p_me * la - (e * p_me + g * p_e) * lh)
        for t in range(LEV // 8):
            lo = t * 8
            a8 = a_sub[lo:lo + 8]
            line = [zbuf[k, pl.ds(lo * BX + x, 8, stride=BX), :] for x in range(BX)]
            for carry, order in ((c1, 1), (d1, -1), (c2, 1), (d2, -1)):
                run = carry[lo:lo + 8]
                for x in range(BX)[::order]:
                    run = a8 * run + line[x]
                    line[x] = run
            for x in range(BX):
                fbuf[k, x, lo:lo + 8, :] = line[x]

    alpha = lx_rate / (1.0 + a_sub)
    scale = 2.0 * lx_rate * lx_rate * lx_rate * alpha * alpha
    pid = iota((LEV, LEV), 0)
    lid = iota((LEV, LEV), 1)
    keep = jnp.abs(pid - lid) <= bands[...]
    mixed = jnp.where(keep, weights[...], 0.0) * scale[:, 0:LEV]
    mh, ml = split(mixed.T)
    mcat = jnp.concatenate([mh, mh, ml], axis=1)
    loads[2].wait()

    def mix(x, carry):
        for k in range(KLOC):
            fh, fl = split(fbuf[k, x])
            fcat = jnp.concatenate([fh, fl, fh], axis=0)
            out_v[k, pl.ds(x, LEV, stride=BX), :] = dot(mcat, fcat, NN)
        return carry

    lax.fori_loop(0, BX, mix, 0, unroll=2)
    stores = []
    for k in range(KLOC):
        out_v[k] = out_v[k] + ctl_v[k].astype(F32)
        cp = pltpu.make_async_copy(out_v.at[k], out.at[k], in_sem.at[3 + k])
        cp.start()
        stores.append(cp)
    for cp in stores:
        cp.wait()


def per_device(members, gradient, control, filter_rates, vertical_weights, band_widths):
    any_ = pl.BlockSpec(memory_space=pl.ANY)
    vm = pl.BlockSpec(memory_space=pltpu.VMEM)
    dma = pltpu.SemaphoreType.DMA
    out = pl.pallas_call(
        kernel,
        out_shape=jax.ShapeDtypeStruct((KLOC, ROWS, BY), F32),
        in_specs=[pl.BlockSpec(memory_space=pltpu.SMEM), vm, vm, vm, any_, any_, any_],
        out_specs=any_,
        scratch_shapes=[
            pltpu.VMEM((KLOC, ROWS, BY), BF16),
            pltpu.VMEM((ROWS, BY), F32),
            pltpu.VMEM((KLOC, ROWS, BY), BF16),
            pltpu.VMEM((KLOC, ROWS, BY), F32),
            pltpu.VMEM((ROWS, BY), F32),
            pltpu.VMEM((ROWS, BY), F32),
            pltpu.VMEM((3, QUARTER, BY), F32),
            pltpu.VMEM((KLOC, ROWS, BY), F32),
            pltpu.VMEM((KLOC, ROWS, BY), F32),
            pltpu.VMEM((LEV * 8, 128), F32),
            pltpu.VMEM((LEV, 128), F32),
            pltpu.VMEM((LEV * BY, BY), BF16),
            pltpu.VMEM((LEV * BY, BY), BF16),
            pltpu.VMEM((GROUPS * 8, 128), F32),
            pltpu.VMEM((4, GROUPS, 128), F32),
            pltpu.VMEM((3, 2, GROUPS, 128), F32),
            pltpu.VMEM((4, GROUPS, 128), F32),
            pltpu.VMEM((4, GROUPS, 128), F32),
            pltpu.VMEM((GROUPS * 8, 128), F32),
            pltpu.VMEM((KLOC, 4, LEV, 128), F32),
            pltpu.VMEM((4, LEV, 128), F32),
            pltpu.VMEM((2, 2, LEV, 128), F32),
            pltpu.VMEM((2, 2, LEV, 128), F32),
            pltpu.VMEM((2, 2, LEV, 128), F32),
            pltpu.VMEM((2, 2, LEV, 128), F32),
            pltpu.VMEM((KLOC, BX, LEV, BY), F32),
            dma((5,)),
            dma((3,)), dma((3,)), dma((3,)), dma((3,)), dma((3,)), dma((3,)),
            dma, dma, dma, dma,
            dma((2, CHUNKS)), dma((2, CHUNKS)), dma((2,)), dma((2,)),
        ],
        compiler_params=pltpu.CompilerParams(
            collective_id=0, has_side_effects=True, vmem_limit_bytes=44 << 20),
        name="localize",
    )(
        filter_rates, filter_rates.reshape(1, LEV), band_widths.reshape(1, LEV), vertical_weights,
        members.reshape(KLOC, ROWS, BY), gradient.reshape(ROWS, BY), control.reshape(KLOC, ROWS, BY),
    )
    return out.reshape(KLOC, LEV, BX, BY)


def solution(mesh):
    placed = (
        P("mem", None, "gx", "gy"),
        P(None, "gx", "gy"),
        P("mem", None, "gx", "gy"),
        P(),
        P(),
        P(),
    )
    return jax.shard_map(
        per_device,
        mesh=mesh,
        in_specs=placed,
        out_specs=P("mem", None, "gx", "gy"),
        check_vma=False,
    )
```

profile of v0, /device:TPU:1, one launch (start us, length us, event | category | flops | bytes accessed | tf_op | source)
XLA Modules:
  0.0 82.0 jit_solution(1859526286514759521)
XLA Ops:
  0.0 0.0 copy-start.4
  0.0 0.0 copy-start.5
  0.0 0.7 copy-done.4
  0.7 0.0 copy-done.5
  0.7 0.0 copy-start
  0.7 1.0 %copy-done = bf16[2,64,16,128]{3,2,1,0:T(8,128)(2,1)S(1)} copy-done((bf16[2,64,16,128]{3,2,1,0:T(8,128)(2,1)S(1)}, bf16[2,64,16,128]{3,2,1,0:T(8,128)(2,1)}, u32[]{:S(2)}) %copy-start) | copy-done | bytes 524312
  1.7 0.0 copy-start.1
  1.7 1.0 %copy-done.1 = f32[64,16,128]{2,1,0:T(8,128)S(1)} copy-done((f32[64,16,128]{2,1,0:T(8,128)S(1)}, f32[64,16,128]{2,1,0:T(8,128)}, u32[]{:S(2)}) %copy-start.1) | copy-done | bytes 524312
  2.8 0.0 copy-start.2
  2.8 1.0 %copy-done.2 = bf16[2,64,16,128]{3,2,1,0:T(8,128)(2,1)S(1)} copy-done((bf16[2,64,16,128]{3,2,1,0:T(8,128)(2,1)S(1)}, bf16[2,64,16,128]{3,2,1,0:T(8,128)(2,1)}, u32[]{:S(2)}) %copy-start.2) | copy-done | bytes 524312
  3.8 0.0 copy-start.3
  3.8 0.8 copy-done.3
  4.6 76.5 %localize.1 = f32[2,1024,128]{2,1,0:T(8,128)S(1)} custom-call(f32[64]{0:T(128)S(1)} %copy-done.4, f32[1,64]{1,0:T(1,128)S(1)} %bitcast.10, s32[1,64]{1,0:T(1,128)S(1)} %bitcast.11, f32[64,64]{1,0:T(8,128)S(1)} %copy-done.3, bf16[2,1024,128]{2,1,0:T(8,128)(2,1)S(1)} %bitcast.7, f32[1024,128]{1,0:T(8,128)S(1)} %bitcast.8, bf16[2,1024,128]{2,1,0:T(8,128)(2,1)S(1)} %bitcast.9), custom_call_target="tpu_custom_call" | custom-call | tf_op jit(solution)/shard_map/localize/pallas_call | solution.py:422
  81.0 1.0 %copy.8 = f32[2,64,16,128]{3,2,1,0:T(8,128)} copy(f32[2,64,16,128]{3,2,1,0:T(8,128)S(1)} %bitcast.6) | data formatting | bytes 2097152
Async XLA Ops:
  0.0 0.7 copy-start.4
  0.0 0.7 copy-start.5
  0.7 1.0 %copy-start = (bf16[2,64,16,128]{3,2,1,0:T(8,128)(2,1)S(1)}, bf16[2,64,16,128]{3,2,1,0:T(8,128)(2,1)}, u32[]{:S(2)}) copy-start(bf16[2,64,16,128]{3,2,1,0:T(8,128)(2,1)} %param.6) | copy-start | bytes 1572868
  1.7 1.0 %copy-start.1 = (f32[64,16,128]{2,1,0:T(8,128)S(1)}, f32[64,16,128]{2,1,0:T(8,128)}, u32[]{:S(2)}) copy-start(f32[64,16,128]{2,1,0:T(8,128)} %param.7) | copy-start | bytes 1572868
  2.8 1.0 %copy-start.2 = (bf16[2,64,16,128]{3,2,1,0:T(8,128)(2,1)S(1)}, bf16[2,64,16,128]{3,2,1,0:T(8,128)(2,1)}, u32[]{:S(2)}) copy-start(bf16[2,64,16,128]{3,2,1,0:T(8,128)(2,1)} %param.8) | copy-start | bytes 1572868
  3.8 0.8 copy-start.3
where the time goes:
time: 82.3 us; the launch traced here: 82 us
  Pallas kernels  76.5 us (93%)
  local copies, waits for them, and re-layouts  5.52 us (7%)
    pallas_call x1, Pallas kernels, per_device(): pl.pallas_call(kernel, out_shape=jax.ShapeDtypeStruct((KLOC, ROWS, BY), F...  76.5 us
    unnamed x13, local copies, waits for them, and re-layouts  5.52 us

commit v1 on v0

v1 whole, which is shorter than its diff:
```python
import functools

import jax
import jax.numpy as jnp
from jax import lax
from jax.experimental import pallas as pl
from jax.experimental.pallas import tpu as pltpu
from jax.sharding import PartitionSpec as P

MESH = pl.DeviceIdType.MESH
F32 = jnp.float32
BF16 = jnp.bfloat16

LEV, MEMBERS, NX, NY = 64, 8, 256, 1024
MEM, GX, GY = 4, 16, 8
KLOC = MEMBERS // MEM
BX, BY = NX // GX, NY // GY
ROWS = LEV * BX
GROUPS = LEV // 4
QUARTER = ROWS // MEM
CHUNKS = 4
CHUNK = LEV // CHUNKS
T1, T2 = 16, 32

NT = (((1,), (1,)), ((), ()))
NN = (((1,), (0,)), ((), ()))
TN = (((0,), (0,)), ((), ()))


def dot(a, b, dims):
    return lax.dot_general(a, b, dims, preferred_element_type=F32)


def split(x):
    hi = x.astype(BF16)
    return hi, (x - hi.astype(F32)).astype(BF16)


def iota(shape, axis):
    return lax.broadcasted_iota(jnp.int32, shape, axis)


def log_decay(r):
    return -r * (1.0 + r * (0.5 + r * (1.0 / 3 + r * (0.25 + r * (0.2 + r * (1.0 / 6))))))


class Line:
    def __init__(self, rate, total, size, index):
        r = rate
        self.rate = r
        self.log = log_decay(r)
        self.a = 1.0 - r
        self.g = self.a * self.a / (r * (1.0 + self.a))
        self.s = (index * size).astype(F32)
        self.last = self.s + (size - 1.0)
        self.n2 = 2.0 * total - self.last
        self.p_s = self.power(self.s)
        self.p_inv = self.power(-self.last)
        self.p_n2 = self.power(self.n2)
        self.ga = self.g * self.power(2.0 * total)
        self.G = 1.0 + 2.0 * self.g + self.ga
        self.total = total
        self.e = self.s + size

    def reach(self, t):
        near = t + self.g + self.ga - self.g * self.power(2.0 * (self.total - t))
        far = self.g * (self.power(-t - 1.0) - self.power(t - 1.0))
        return near, far

    def power(self, m):
        return jnp.exp(self.log * m)

    def sums(self, r1, r2, q1, q2):
        sa = self.p_inv * r1
        fq = self.p_s * q1
        sb = self.p_inv * (self.last * r1 - r2) + self.g * fq
        lh = fq - self.p_n2 * r1
        la = self.p_s * ((self.s + self.G) * q1 + q2) - self.p_n2 * ((self.n2 + self.G) * r1 + r2)
        return sa, sb, la, lh


def kernel(rates_h, bands_h, weights_h, members, gradient, control, out,
           rates, bands, weights, mem_v, grad_v, ctl_v, psum, total, rs_rcv, vbuf, zbuf, wtab, lsub, thi, tlo,
           mu, ysum, yone, xsum, xrs, xmn, ysnd, yrcv, zsnd, zrcv, kap, xst, xpair, xin, xout, xss, xsr,
           cown, csib, ctot, crcv, xr, xf, fbuf,
           in_sem, rs_s, rs_r, ag_s, ag_r, o_s, o_r, xs_s, xs_r, xa_s, xa_r, y_s, y_r, h_s, h_r, p_s, p_r,
           c_s, c_r, d_s, d_r, k_s, k_r, l_s, l_r):
    i = lax.axis_index("mem")
    gx = lax.axis_index("gx")
    gy = lax.axis_index("gy")
    z, core = gx // 2, gx % 2
    yy, hh = gy // 2, gy % 2

    barrier = pltpu.get_barrier_semaphore()

    def signal(dev):
        pl.semaphore_signal(barrier, inc=1, device_id=dev, device_id_type=MESH)

    sibling = (i, gx + 1 - 2 * core, gy)
    across = (i, gx, gy + 1 - 2 * hh)
    peers = [((i + d) % MEM, gx, gy) for d in range(1, MEM)]
    y_at = [(yy + d) % 4 for d in range(1, 4)]
    chips = [(i, ((z + d) % 8) * 2 + core, gy) for d in range(1, 8)]
    signal(across)
    for dev in chips[2:5] + chips[1:2] + chips[5:6] + chips[0:1] + chips[6:7]:
        signal(dev)
    for d in range(3):
        signal(peers[d])
        signal((i, gx, y_at[d] * 2 + hh))
    signal(sibling)

    loads = [
        pltpu.make_async_copy(rates_h, rates, in_sem.at[0]),
        pltpu.make_async_copy(members, mem_v, in_sem.at[1]),
        pltpu.make_async_copy(gradient, grad_v, in_sem.at[2]),
        pltpu.make_async_copy(weights_h, weights, in_sem.at[3]),
        pltpu.make_async_copy(bands_h, bands, in_sem.at[4]),
        pltpu.make_async_copy(control, ctl_v, in_sem.at[5]),
    ]
    for load in loads:
        load.start()

    def remote(src, dst, ss, rs, dev):
        return pltpu.make_async_remote_copy(
            src_ref=src, dst_ref=dst, send_sem=ss, recv_sem=rs, device_id=dev, device_id_type=MESH)

    loads[0].wait()
    sub8 = iota((8, 128), 0)
    for t in range(LEV // 8):
        v = jnp.zeros((8, 128), F32)
        for j in range(8):
            v = jnp.where(sub8 == j, rates[t * 8 + j], v)
        lsub[t * 8:(t + 1) * 8, :] = v
    lane = iota((GROUPS, 128), 1)
    lev_id = iota((GROUPS, 128), 0) * 4 + (lane // BX) % 4
    rate_lane = jnp.zeros((GROUPS, 128), F32)
    for l in range(LEV):
        rate_lane = jnp.where(lev_id == l, rates[l], rate_lane)
    ly = Line(rate_lane, NY, BY, gy)
    lx = Line(lsub[...], NX, BX, gx)
    a_sub = lx.a

    cell = iota((8, 128), 1).astype(F32)
    kind = sub8 % 4
    dist = jnp.where(kind < 2, 127.0 - cell, cell)
    factor = jnp.where(kind % 2 == 0, 1.0, dist)

    def basis(l, carry):
        lg = log_decay(jnp.broadcast_to(lsub[pl.ds(l, 1), :], (8, 128)))
        wtab[pl.ds(pl.multiple_of(l * 8, 8), 8), :] = jnp.exp(dist * lg) * factor
        return carry

    lax.fori_loop(0, LEV, basis, 0, unroll=8)

    loads[1].wait()
    loads[2].wait()
    lane8 = (iota((8, 128), 1) // BX) % 4

    def product(g, carry):
        at = pl.multiple_of(g * 64, 64)
        gr = grad_v[pl.ds(at, 64), :]
        m0 = mem_v[0, pl.ds(at, 64), :].astype(F32)
        m1 = mem_v[1, pl.ds(at, 64), :].astype(F32)
        psum[pl.ds(at, 64), :] = m0 + m1
        v0 = m0 * gr
        v1 = m1 * gr
        vbuf[0, pl.ds(at, 64), :] = v0
        vbuf[1, pl.ds(at, 64), :] = v1
        vh, vl = split(jnp.concatenate([v0, v1], axis=0))
        wh, wl = split(wtab[pl.ds(pl.multiple_of(g * 32, 32), 32), :])
        res = dot(wh, vh, NT) + dot(wh, vl, NT) + dot(wl, vh, NT)
        m8 = jnp.zeros((8, 128), F32)
        for lv in range(4):
            m8 = jnp.where(lane8 == lv, res[lv * 8:lv * 8 + 8, :], m8)
        mu[pl.ds(pl.multiple_of(g * 8, 8), 8), :] = m8
        return carry

    lax.fori_loop(0, GROUPS, product, 0, unroll=2)
    ymom = [mu[pl.ds(q, GROUPS, stride=8), :] for q in range(4)]
    low = lane < 64
    two = [m + pltpu.roll(m, 64, 1) for m in ymom]
    ysum[0] = jnp.where(low, two[0], two[1])
    ysum[1] = jnp.where(low, two[2], two[3])

    pl.semaphore_wait(barrier, 15)
    one = [remote(ysum, yone.at[d], o_s.at[d], o_r.at[d], peers[d]) for d in range(3)]
    for cp in one:
        cp.start()

    for k in range(KLOC):
        r1 = jnp.zeros((LEV, 128), F32)
        r2, q1, q2 = r1, r1, r1
        for x in range(BX):
            v = vbuf[k, pl.ds(x, LEV, stride=BX), :]
            t = a_sub * r1
            r2 = a_sub * r2 + t
            r1 = t + v
            v = vbuf[k, pl.ds(BX - 1 - x, LEV, stride=BX), :]
            t = a_sub * q1
            q2 = a_sub * q2 + t
            q1 = t + v
        for q, s in enumerate(lx.sums(r1, r2, q1, q2)):
            xst[k, q] = s
            if k == 1:
                xsum[q] = xst[0, q] + s
    own16 = pl.multiple_of(i * 16, 16)
    xrc = [remote(xsum.at[:, pl.ds(pl.multiple_of(peers[d][0] * 16, 16), 16)], xrs.at[d],
                  xs_s.at[d], xs_r.at[d], peers[d]) for d in range(3)]
    for cp in xrc:
        cp.start()
    rs = [remote(psum.at[pl.ds(pl.multiple_of(peers[d][0] * QUARTER, QUARTER), QUARTER)], rs_rcv.at[d],
                 rs_s.at[d], rs_r.at[d], peers[d]) for d in range(3)]
    for cp in rs:
        cp.start()

    di = jnp.abs(iota((BY, BY), 0) - iota((BY, BY), 1)).astype(F32)

    def toeplitz(l, carry):
        r = jnp.broadcast_to(lsub[pl.ds(l, 1), :], (8, 128))
        lg = log_decay(r)
        a = 1.0 - r
        c = 1.0 + 2.0 * (a * a / (r * (1.0 + a)))
        lg = jnp.broadcast_to(lg[0:1, :], (BY, BY))
        c = jnp.broadcast_to(c[0:1, :], (BY, BY))
        hi, lo = split(jnp.exp(di * lg) * (di + c))
        at = pl.multiple_of(l * BY, BY)
        thi[pl.ds(at, BY), :] = hi
        tlo[pl.ds(at, BY), :] = lo
        return carry

    lax.fori_loop(0, T1, toeplitz, 0)

    for cp in one:
        cp.wait()
    tot = [ysum[j] + yone[0, j] + yone[1, j] + yone[2, j] for j in range(2)]
    swap = [pltpu.roll(t, 64, 1) for t in tot]
    mean = [jnp.where(low, tot[0], swap[0]), jnp.where(low, swap[0], tot[0]),
            jnp.where(low, tot[1], swap[1]), jnp.where(low, swap[1], tot[1])]
    r1, r2, q1, q2 = [m - t * (1.0 / MEMBERS) for m, t in zip(ymom, mean)]
    own_y = ly.sums(r1, r2, q1, q2)
    for q in range(4):
        ysnd[q] = own_y[q]
    ycp = []
    for d in range(3):
        part = pl.multiple_of(jnp.where(y_at[d] > yy, 0, 2), 2)
        cp = remote(ysnd.at[pl.ds(part, 2)], yrcv.at[d], y_s.at[d], y_r.at[d], (i, gx, y_at[d] * 2 + hh))
        cp.start()
        ycp.append(cp)

    for cp in xrc:
        cp.wait()
    xmn[:, pl.ds(own16, 16)] = (xsum[:, pl.ds(own16, 16)] + xrs[0] + xrs[1] + xrs[2]) * (1.0 / MEMBERS)
    xag = [remote(xmn.at[:, pl.ds(own16, 16)], xmn.at[:, pl.ds(own16, 16)], xa_s.at[d], xa_r.at[d], peers[d])
           for d in range(3)]
    for cp in xag:
        cp.start()
    lax.fori_loop(T1, T2, toeplitz, 0)

    for cp in ycp:
        cp.wait()
    zero = jnp.zeros((GROUPS, 128), F32)
    sa = sb = la = lh = zero
    for d in range(3):
        from_left = (yy - (d + 1)) >= 0
        u, w = yrcv[d, 0], yrcv[d, 1]
        sa = sa + jnp.where(from_left, u, 0.0)
        sb = sb + jnp.where(from_left, w, 0.0)
        la = la + jnp.where(from_left, 0.0, u)
        lh = lh + jnp.where(from_left, 0.0, w)
    zsnd[0] = sa + jnp.where(hh == 0, own_y[0], 0.0)
    zsnd[1] = sb + jnp.where(hh == 0, own_y[1], 0.0)
    zsnd[2] = la + jnp.where(hh == 1, own_y[2], 0.0)
    zsnd[3] = lh + jnp.where(hh == 1, own_y[3], 0.0)
    hcp = remote(zsnd, zrcv, h_s, h_r, across)
    hcp.start()

    for cp in xag:
        cp.wait()
    for k in range(KLOC):
        xst[k] = xst[k] - xmn[...]
    pcp = remote(xst.at[1 - core], xpair, p_s, p_r, sibling)
    pcp.start()

    own = pl.multiple_of(i * QUARTER, QUARTER)
    for cp in rs:
        cp.wait()
    total[pl.ds(own, QUARTER), :] = (psum[pl.ds(own, QUARTER), :] + rs_rcv[0]
                                     + rs_rcv[1] + rs_rcv[2])
    ag = [remote(total.at[pl.ds(own, QUARTER)], total.at[pl.ds(own, QUARTER)], ag_s.at[d], ag_r.at[d], peers[d])
          for d in range(3)]
    for cp in ag:
        cp.start()
    pcp.wait()

    def chain(turn):
        way = ((z >= 4).astype(jnp.int32) + turn) % 2
        has_in = jnp.where(way == 0, z > 0, z < 7)
        has_out = jnp.where(way == 0, z < 7, z > 0)
        target = (i, gx + 2 - 4 * way, gy)
        part = pl.multiple_of(way * 2, 2)

        def copy(c):
            rows = pl.ds(c * CHUNK, CHUNK)
            return remote(xout.at[way, :, rows], xin.at[way, :, rows], c_s.at[way, c], c_r.at[way, c], target)

        @pl.when(jnp.logical_not(has_in))
        def _():
            xin[way] = jnp.zeros((2, LEV, 128), F32)

        for c in range(CHUNKS):
            rows = slice(c * CHUNK, (c + 1) * CHUNK)

            @pl.when(has_in)
            def _():
                copy(c).wait_recv()

            @pl.when(has_out)
            def _():
                xout[way, :, rows] = (xin[way, :, rows] + xst[core, pl.ds(part, 2), rows]
                                      + xpair[pl.ds(part, 2), rows])
                copy(c).start()

        add = jnp.where(way == core, 1.0, 0.0)
        xss[way] = xin[way] + add * xst[core, pl.ds(part, 2)]
        sib = remote(xss.at[way], xsr.at[way], d_s.at[way], d_r.at[way], sibling)
        sib.start()
        xin[way] = xin[way] + (1.0 - add) * xpair[pl.ds(part, 2)]
        return way, has_out, copy, sib

    def drain(done):
        for way, has_out, copy, sib in done:
            sib.wait()
            for c in range(CHUNKS):
                @pl.when(has_out)
                def _():
                    copy(c).wait_send()

    done = [chain(0)]

    hcp.wait()
    sa = sa + zrcv[0]
    sb = sb + zrcv[1]
    la = la + zrcv[2]
    lh = lh + zrcv[3]
    k1 = (ly.p_n2 * (sb - sa * (ly.n2 + ly.G)) + ly.p_inv * (la - lh * ly.last)
          + ly.ga * ly.p_inv * (ly.p_s * q1)
          - ly.p_n2 * ly.p_inv * ((2.0 * (NY - ly.last) + ly.G) * r1 + r2))
    k2 = lh * ly.p_inv - sa * ly.p_n2 - ly.p_n2 * ly.p_inv * r1
    k3 = ly.p_s * (sa * (ly.s + ly.G) - sb - lh * ly.g + ly.ga * ly.p_inv * r1 - ly.g * ly.p_s * q1)
    k4 = sa * ly.p_s
    kk = (k1, k2, k3, k4)

    lxl = Line(rate_lane, NX, BX, gx)
    xc = (lane % BX).astype(F32)
    up, down = lxl.power(xc), lxl.power(BX - 1.0 - xc)
    wts = lxl.sums(down, (BX - 1.0 - xc) * down, up, xc * up)
    stack = jnp.concatenate([w * kq for w in wts for kq in kk], axis=0)
    seg = (iota((128, 128), 0) // BX == iota((128, 128), 1) // BX).astype(BF16)
    sh, sl = split(stack)
    res = dot(sh, seg, NN) + dot(sl, seg, NN)
    slot = lane % BX
    cor = zero
    for c in range(16):
        cor = jnp.where(slot == c, res[c * GROUPS:(c + 1) * GROUPS], cor)
    cown[...] = cor
    lcp = remote(cown, csib, l_s, l_r, sibling)
    lcp.start()
    for q, k in enumerate(kk + (zero,) * 4):
        kap[pl.ds(q, GROUPS, stride=8), :] = k
    lcp.wait()
    ctot[...] = cor + csib[...]
    ccp = [remote(ctot, crcv.at[d], k_s.at[d], k_r.at[d], chips[d]) for d in range(7)]
    for d in (3, 2, 4, 1, 5, 0, 6):
        ccp[d].start()

    def local_y(l, carry):
        at = pl.multiple_of(l * BX, BX)
        tt = pl.multiple_of(l * BY, BY)
        mean = total[pl.ds(at, BX), :] * (1.0 / MEMBERS)
        gr = grad_v[pl.ds(at, BX), :]
        v = jnp.concatenate([(mem_v[k, pl.ds(at, BX), :].astype(F32) - mean) * gr for k in range(KLOC)], axis=0)
        vh, vl = split(v)
        th = thi[pl.ds(tt, BY), :]
        res = dot(vh, th, NN) + dot(vl, th, NN) + dot(vh, tlo[pl.ds(tt, BY), :], NN)
        zbuf[0, pl.ds(at, BX), :] = res[0:BX]
        zbuf[1, pl.ds(at, BX), :] = res[BX:]
        return carry

    def synth(g, carry):
        at = pl.multiple_of(g * 64, 64)
        k8 = kap[pl.ds(pl.multiple_of(g * 8, 8), 8), :]
        big = jnp.concatenate([jnp.where(lane8 == lv, k8, 0.0) for lv in range(4)], axis=0)
        kh, kl = split(big.T)
        wh, wl = split(wtab[pl.ds(pl.multiple_of(g * 32, 32), 32), :])
        res = dot(kh, wh, NN) + dot(kl, wh, NN) + dot(kh, wl, NN)
        zbuf[0, pl.ds(at, 64), :] += res[0:64]
        zbuf[1, pl.ds(at, 64), :] += res[64:]
        return carry

    def block():
        for cp in ag:
            cp.wait()
        lax.fori_loop(0, LEV, local_y, 0, unroll=2)
        lax.fori_loop(0, GROUPS, synth, 0)

    middle = (z == 3) | (z == 4)
    for load in loads[3:5]:
        load.wait()
    alpha = lx.rate / (1.0 + a_sub)
    scale = 2.0 * lx.rate * lx.rate * lx.rate * alpha * alpha
    pid = iota((LEV, LEV), 0)
    lid = iota((LEV, LEV), 1)
    keep = jnp.abs(pid - lid) <= bands[...]
    mixed = jnp.where(keep, weights[...], 0.0) * scale[:, 0:LEV]
    mh, ml = split(mixed.T)
    mcat = jnp.concatenate([mh, mh, ml], axis=1)

    def rest():
        lax.fori_loop(T2, LEV, toeplitz, 0)
        block()

    @pl.when(jnp.logical_not(middle))
    def _():
        rest()

    done.append(chain(1))

    @pl.when(middle)
    def _():
        rest()

    drain(done)

    for k in range(KLOC):
        for q in range(4):
            row = (k * 4 + q) * LEV
            xr[row:row + LEV, :] = jnp.where(core == k, xin[q // 2, q % 2], xsr[q // 2, q % 2])

    def local_x(l, carry):
        tt = pl.multiple_of(l * BY, BY)
        vh, vl = split(xr[pl.ds(l, 8, stride=LEV), :])
        th = thi[pl.ds(tt, BY), :]
        xf[pl.ds(l, 8, stride=LEV), :] = dot(vh, th, NN) + dot(vl, th, NN) + dot(vh, tlo[pl.ds(tt, BY), :], NN)
        return carry

    lax.fori_loop(0, LEV, local_x, 0, unroll=4)
    for cp in ccp:
        cp.wait()
    right = slot < 8
    cst = jnp.where(right == (core == 1), csib[...], 0.0)
    for d in range(7):
        from_left = (z - (d + 1)) >= 0
        cst = cst + jnp.where(right == from_left, crcv[d], 0.0)
    cown[...] = cst
    zr, zc = iota((64, 256), 0), iota((64, 256), 1)
    fits = ((zr // 32 == (zc // 64) % 2) & ((zr // 8) % 4 == (zc // 4) % 4)
            & ((zr % 8) // 4 == zc // 128) & (zr % 4 == (zc // 16) % 4))

    def synth_x(t, carry):
        row = jnp.concatenate([cown[pl.ds(2 * t, 1), :], cown[pl.ds(2 * t + 1, 1), :]], axis=1)
        kh, kl = split(jnp.where(fits, jnp.broadcast_to(row, (64, 256)), 0.0))
        w = wtab[pl.ds(pl.multiple_of(t * 64, 64), 64), :]
        tiles = [w[(g * 4 + lv) * 8:(g * 4 + lv) * 8 + 8] for g in range(2) for k in range(2)
                 for lv in range(4) for twice in range(2)]
        wh, wl = split(jnp.concatenate(tiles, axis=0))
        res = dot(kh, wh, NN) + dot(kl, wh, NN) + dot(kh, wl, NN)
        for j in range(8):
            xf[pl.ds(pl.multiple_of(j * LEV + t * 8, 8), 8), :] += res[j * 8:(j + 1) * 8]
        return carry

    lax.fori_loop(0, LEV // 8, synth_x, 0)

    g, s, e, G = lx.g, lx.s, lx.e, lx.G
    ge = 1.0 + g
    p_s, p_e, p_me, p_2e = lx.power(s), lx.power(e), lx.power(-e), lx.power(2.0 * NX - e)
    hx = p_e - p_2e
    ux = p_e * (e + G) - p_2e * (2.0 * NX - e + G)
    hs = p_s - lx.power(2.0 * NX - s)
    p_s1, p_1e = lx.power(s - 1.0), lx.power(1.0 - e)
    near_s, far_s = lx.reach(s)
    near_e, far_e = lx.reach(e)

    for k in range(KLOC):
        for t in range(LEV // 8):
            lo = t * 8
            cut = lambda m: m[lo:lo + 8]
            sa, sb, la, lh = [xf[(k * 4 + q) * LEV + lo:(k * 4 + q) * LEV + lo + 8, :] for q in range(4)]
            a8, ge8, hx8, pm8 = cut(a_sub), cut(ge), cut(hx), cut(p_me)
            line = [zbuf[k, pl.ds(lo * BX + x, 8, stride=BX), :] for x in range(BX)]

            def sweep(run, order):
                for x in range(BX)[::order]:
                    run = a8 * run + line[x]
                    line[x] = run
                return run

            sa_e = cut(p_1e) * sweep(cut(p_s1) * sa, 1)
            first = sweep(ge8 * (hx8 * sa_e + pm8 * lh), -1)
            lh_s = cut(p_s) * (first / ge8 - cut(hs) * sa)
            last = sweep(ge8 * (cut(p_s1) * (cut(near_s) * sa - sb) + cut(far_s) * lh_s), 1)
            sb_e = cut(near_e) * sa_e - cut(p_1e) * (last / ge8 - cut(far_e) * lh)
            sweep(ge8 * ge8 * (cut(ux) * sa_e - hx8 * sb_e + pm8 * la - (e * pm8 + cut(g) * cut(p_e)) * lh), -1)
            for x in range(BX):
                fbuf[k, x, lo:lo + 8, :] = line[x]

    def mix(x, carry):
        for k in range(KLOC):
            fh, fl = split(fbuf[k, x])
            fcat = jnp.concatenate([fh, fl, fh], axis=0)
            out[k, pl.ds(x, LEV, stride=BX), :] = dot(mcat, fcat, NN)
        return carry

    lax.fori_loop(0, BX, mix, 0, unroll=2)
    loads[5].wait()
    for k in range(KLOC):
        out[k] = out[k] + ctl_v[k].astype(F32)


def per_device(members, gradient, control, filter_rates, vertical_weights, band_widths):
    hbm = pl.BlockSpec(memory_space=pltpu.HBM)
    dma = pltpu.SemaphoreType.DMA

    def vm(*shape):
        return pltpu.VMEM(shape, F32)

    three = [dma((3,))] * 2
    single = [dma] * 2
    out = pl.pallas_call(
        kernel,
        out_shape=jax.ShapeDtypeStruct((KLOC, ROWS, BY), F32),
        in_specs=[hbm] * 6,
        out_specs=pl.BlockSpec(memory_space=pltpu.VMEM),
        scratch_shapes=[
            pltpu.SMEM((LEV,), F32),
            pltpu.VMEM((1, LEV), jnp.int32),
            vm(LEV, LEV),
            pltpu.VMEM((KLOC, ROWS, BY), BF16),
            vm(ROWS, BY),
            pltpu.VMEM((KLOC, ROWS, BY), BF16),
            vm(ROWS, BY), vm(ROWS, BY), vm(3, QUARTER, BY),
            vm(KLOC, ROWS, BY), vm(KLOC, ROWS, BY),
            vm(LEV * 8, 128), vm(LEV, 128),
            pltpu.VMEM((LEV * BY, BY), BF16),
            pltpu.VMEM((LEV * BY, BY), BF16),
            vm(GROUPS * 8, 128),
            vm(2, GROUPS, 128), vm(3, 2, GROUPS, 128),
            vm(4, LEV, 128), vm(3, 4, 16, 128), vm(4, LEV, 128),
            vm(4, GROUPS, 128), vm(3, 2, GROUPS, 128), vm(4, GROUPS, 128), vm(4, GROUPS, 128),
            vm(GROUPS * 8, 128),
            vm(KLOC, 4, LEV, 128), vm(4, LEV, 128),
            vm(2, 2, LEV, 128), vm(2, 2, LEV, 128), vm(2, 2, LEV, 128), vm(2, 2, LEV, 128),
            vm(GROUPS, 128), vm(GROUPS, 128), vm(GROUPS, 128), vm(7, GROUPS, 128),
            vm(8 * LEV, 128), vm(8 * LEV, 128),
            vm(KLOC, BX, LEV, BY),
            dma((6,)),
            *three, *three, *three, *three, *three, *three,
            *single, *single,
            dma((2, CHUNKS)), dma((2, CHUNKS)), dma((2,)), dma((2,)),
            dma((7,)), dma((7,)), *single,
        ],
        compiler_params=pltpu.CompilerParams(
            collective_id=0, has_side_effects=True, vmem_limit_bytes=60 << 20),
        name="localize",
    )(
        filter_rates, band_widths.reshape(1, LEV), vertical_weights,
        members.reshape(KLOC, ROWS, BY), gradient.reshape(ROWS, BY), control.reshape(KLOC, ROWS, BY),
    )
    return out.reshape(KLOC, LEV, BX, BY)


def solution(mesh):
    placed = (
        P("mem", None, "gx", "gy"),
        P(None, "gx", "gy"),
        P("mem", None, "gx", "gy"),
        P(),
        P(),
        P(),
    )
    return jax.shard_map(
        per_device,
        mesh=mesh,
        in_specs=placed,
        out_specs=P("mem", None, "gx", "gy"),
        check_vma=False,
    )
```

time: 82.3 us -> 67.6 us (0.82)
  Pallas kernels: 76.5 us -> 65.1 us
  local copies, waits for them, and re-layouts: 5.52 us -> 2.26 us
    pallas_call x1, Pallas kernels: 76.5 us -> 65.1 us  [per_device(): pl.pallas_call(kernel, out_shape=jax.ShapeDtypeStruct((KLOC, ROWS, BY), F...]
    unnamed x13 -> x1, local copies, waits for them, and re-layouts: 5.52 us -> 2.26 us
where the time goes in v1:
time: 67.6 us; the launch traced here: 67.4 us
  Pallas kernels  65.1 us (96%)
  local copies, waits for them, and re-layouts  2.26 us (3%)
    pallas_call x1, Pallas kernels, per_device(): pl.pallas_call(kernel, out_shape=jax.ShapeDtypeStruct((KLOC, ROWS, BY), F...  65.1 us
    unnamed x1, local copies, waits for them, and re-layouts  2.26 us

profile of v1, /device:TPU:1, one launch (start us, length us, event | category | flops | bytes accessed | tf_op | source)
XLA Modules:
  0.0 67.4 jit_solution(144124789408244823)
XLA Ops:
  0.0 65.1 %localize.1 = f32[2,1024,128]{2,1,0:T(8,128)} custom-call(f32[64]{0:T(128)} %rates_h.1, s32[1,64]{1,0:T(1,128)} %bitcast.9, f32[64,64]{1,0:T(8,128)} %weights_h.1, bf16[2,1024,128]{2,1,0:T(8,128)(2,1)} %bitcast.6, f32[1024,128]{1,0:T(8,128)} %bitcast.7, bf16[2,1024,128]{2,1,0:T(8,128)(2,1)} %bitcast.8), custom_call_target="tpu_custom_call" | custom-call | tf_op jit(solution)/shard_map/localize/pallas_call | solution.py:528
  65.2 2.3 %copy.8 = f32[2,64,16,128]{3,2,1,0:T(8,128)} copy(f32[2,64,16,128]{3,2,1,0:T(8,128)} %bitcast.5) | data formatting | bytes 2097152

commit v2 on v1

--- a/solution.py
+++ b/solution.py
@@ -20,7 +20,6 @@
 QUARTER = ROWS // MEM
 CHUNKS = 4
 CHUNK = LEV // CHUNKS
-T1, T2 = 16, 32
 
 NT = (((1,), (1,)), ((), ()))
 NN = (((1,), (0,)), ((), ()))
@@ -79,8 +78,8 @@
         return sa, sb, la, lh
 
 
-def kernel(rates_h, bands_h, weights_h, members, gradient, control, out,
-           rates, bands, weights, mem_v, grad_v, ctl_v, psum, total, rs_rcv, vbuf, zbuf, wtab, lsub, thi, tlo,
+def kernel(rates_h, bands_h, weights_h, members, gradient, out,
+           rates, bands, weights, mem_v, grad_v, psum, total, rs_rcv, vbuf, zbuf, wtab, lsub, thi, tlo,
            mu, ysum, yone, xsum, xrs, xmn, ysnd, yrcv, zsnd, zrcv, kap, xst, xpair, xin, xout, xss, xsr,
            cown, csib, ctot, crcv, xr, xf, fbuf,
            in_sem, rs_s, rs_r, ag_s, ag_r, o_s, o_r, xs_s, xs_r, xa_s, xa_r, y_s, y_r, h_s, h_r, p_s, p_r,
@@ -115,7 +114,6 @@
         pltpu.make_async_copy(gradient, grad_v, in_sem.at[2]),
         pltpu.make_async_copy(weights_h, weights, in_sem.at[3]),
         pltpu.make_async_copy(bands_h, bands, in_sem.at[4]),
-        pltpu.make_async_copy(control, ctl_v, in_sem.at[5]),
     ]
     for load in loads:
         load.start()
@@ -175,7 +173,7 @@
         mu[pl.ds(pl.multiple_of(g * 8, 8), 8), :] = m8
         return carry
 
-    lax.fori_loop(0, GROUPS, product, 0, unroll=2)
+    lax.fori_loop(0, GROUPS, product, 0, unroll=GROUPS)
     ymom = [mu[pl.ds(q, GROUPS, stride=8), :] for q in range(4)]
     low = lane < 64
     two = [m + pltpu.roll(m, 64, 1) for m in ymom]
@@ -228,7 +226,7 @@
         tlo[pl.ds(at, BY), :] = lo
         return carry
 
-    lax.fori_loop(0, T1, toeplitz, 0)
+    lax.fori_loop(0, LEV, toeplitz, 0, unroll=2)
 
     for cp in one:
         cp.wait()
@@ -254,7 +252,6 @@
            for d in range(3)]
     for cp in xag:
         cp.start()
-    lax.fori_loop(T1, T2, toeplitz, 0)
 
     for cp in ycp:
         cp.wait()
@@ -281,6 +278,52 @@
     pcp = remote(xst.at[1 - core], xpair, p_s, p_r, sibling)
     pcp.start()
 
+    pcp.wait()
+
+    def chain(turn):
+        way = ((z >= 4).astype(jnp.int32) + turn) % 2
+        has_in = jnp.where(way == 0, z > 0, z < 7)
+        has_out = jnp.where(way == 0, z < 7, z > 0)
+        target = (i, gx + 2 - 4 * way, gy)
+        part = pl.multiple_of(way * 2, 2)
+
+        def copy(c):
+            rows = pl.ds(c * CHUNK, CHUNK)
+            return remote(xout.at[way, :, rows], xin.at[way, :, rows], c_s.at[way, c], c_r.at[way, c], target)
+
+        @pl.when(jnp.logical_not(has_in))
+        def _():
+            xin[way] = jnp.zeros((2, LEV, 128), F32)
+
+        for c in range(CHUNKS):
+            rows = slice(c * CHUNK, (c + 1) * CHUNK)
+
+            @pl.when(has_in)
+            def _():
+                copy(c).wait_recv()
+
+            @pl.when(has_out)
+            def _():
+                xout[way, :, rows] = (xin[way, :, rows] + xst[core, pl.ds(part, 2), rows]
+                                      + xpair[pl.ds(part, 2), rows])
+                copy(c).start()
+
+        add = jnp.where(way == core, 1.0, 0.0)
+        xss[way] = xin[way] + add * xst[core, pl.ds(part, 2)]
+        sib = remote(xss.at[way], xsr.at[way], d_s.at[way], d_r.at[way], sibling)
+        sib.start()
+        xin[way] = xin[way] + (1.0 - add) * xpair[pl.ds(part, 2)]
+        return way, has_out, copy, sib
+
+    def drain(done):
+        for way, has_out, copy, sib in done:
+            sib.wait()
+            for c in range(CHUNKS):
+                @pl.when(has_out)
+                def _():
+                    copy(c).wait_send()
+
+    done = [chain(0)]
     own = pl.multiple_of(i * QUARTER, QUARTER)
     for cp in rs:
         cp.wait()
@@ -290,52 +333,6 @@
           for d in range(3)]
     for cp in ag:
         cp.start()
-    pcp.wait()
-
-    def chain(turn):
-        way = ((z >= 4).astype(jnp.int32) + turn) % 2
-        has_in = jnp.where(way == 0, z > 0, z < 7)
-        has_out = jnp.where(way == 0, z < 7, z > 0)
-        target = (i, gx + 2 - 4 * way, gy)
-        part = pl.multiple_of(way * 2, 2)
-
-        def copy(c):
-            rows = pl.ds(c * CHUNK, CHUNK)
-            return remote(xout.at[way, :, rows], xin.at[way, :, rows], c_s.at[way, c], c_r.at[way, c], target)
-
-        @pl.when(jnp.logical_not(has_in))
-        def _():
-            xin[way] = jnp.zeros((2, LEV, 128), F32)
-
-        for c in range(CHUNKS):
-            rows = slice(c * CHUNK, (c + 1) * CHUNK)
-
-            @pl.when(has_in)
-            def _():
-                copy(c).wait_recv()
-
-            @pl.when(has_out)
-            def _():
-                xout[way, :, rows] = (xin[way, :, rows] + xst[core, pl.ds(part, 2), rows]
-                                      + xpair[pl.ds(part, 2), rows])
-                copy(c).start()
-
-        add = jnp.where(way == core, 1.0, 0.0)
-        xss[way] = xin[way] + add * xst[core, pl.ds(part, 2)]
-        sib = remote(xss.at[way], xsr.at[way], d_s.at[way], d_r.at[way], sibling)
-        sib.start()
-        xin[way] = xin[way] + (1.0 - add) * xpair[pl.ds(part, 2)]
-        return way, has_out, copy, sib
-
-    def drain(done):
-        for way, has_out, copy, sib in done:
-            sib.wait()
-            for c in range(CHUNKS):
-                @pl.when(has_out)
-                def _():
-                    copy(c).wait_send()
-
-    done = [chain(0)]
 
     hcp.wait()
     sa = sa + zrcv[0]
@@ -367,11 +364,14 @@
     lcp.start()
     for q, k in enumerate(kk + (zero,) * 4):
         kap[pl.ds(q, GROUPS, stride=8), :] = k
-    lcp.wait()
-    ctot[...] = cor + csib[...]
+
+    def spread():
+        lcp.wait()
+        ctot[...] = cor + csib[...]
+        for d in (3, 2, 4, 1, 5, 0, 6):
+            ccp[d].start()
+
     ccp = [remote(ctot, crcv.at[d], k_s.at[d], k_r.at[d], chips[d]) for d in range(7)]
-    for d in (3, 2, 4, 1, 5, 0, 6):
-        ccp[d].start()
 
     def local_y(l, carry):
         at = pl.multiple_of(l * BX, BX)
@@ -379,9 +379,10 @@
         mean = total[pl.ds(at, BX), :] * (1.0 / MEMBERS)
         gr = grad_v[pl.ds(at, BX), :]
         v = jnp.concatenate([(mem_v[k, pl.ds(at, BX), :].astype(F32) - mean) * gr for k in range(KLOC)], axis=0)
-        vh, vl = split(v)
-        th = thi[pl.ds(tt, BY), :]
-        res = dot(vh, th, NN) + dot(vl, th, NN) + dot(vh, tlo[pl.ds(tt, BY), :], NN)
+        n = KLOC * BX
+        both = jnp.concatenate([thi[pl.ds(tt, BY), :], tlo[pl.ds(tt, BY), :]], axis=1)
+        res = dot(jnp.concatenate(split(v), axis=0), both, NN)
+        res = res[:n, :BY] + res[n:, :BY] + res[:n, BY:]
         zbuf[0, pl.ds(at, BX), :] = res[0:BX]
         zbuf[1, pl.ds(at, BX), :] = res[BX:]
         return carry
@@ -390,9 +391,9 @@
         at = pl.multiple_of(g * 64, 64)
         k8 = kap[pl.ds(pl.multiple_of(g * 8, 8), 8), :]
         big = jnp.concatenate([jnp.where(lane8 == lv, k8, 0.0) for lv in range(4)], axis=0)
-        kh, kl = split(big.T)
+        kh, kl = split(big)
         wh, wl = split(wtab[pl.ds(pl.multiple_of(g * 32, 32), 32), :])
-        res = dot(kh, wh, NN) + dot(kl, wh, NN) + dot(kh, wl, NN)
+        res = dot(jnp.concatenate([kh, kl, kh], axis=0), jnp.concatenate([wh, wh, wl], axis=0), TN)
         zbuf[0, pl.ds(at, 64), :] += res[0:64]
         zbuf[1, pl.ds(at, 64), :] += res[64:]
         return carry
@@ -400,10 +401,16 @@
     def block():
         for cp in ag:
             cp.wait()
-        lax.fori_loop(0, LEV, local_y, 0, unroll=2)
-        lax.fori_loop(0, GROUPS, synth, 0)
-
-    middle = (z == 3) | (z == 4)
+        lax.fori_loop(0, LEV, local_y, 0, unroll=8)
+        lax.fori_loop(0, GROUPS, synth, 0, unroll=4)
+
+    middle = (z >= 2) & (z <= 5)
+    centre = (z == 3) | (z == 4)
+
+    @pl.when(jnp.logical_not(centre))
+    def _():
+        spread()
+
     for load in loads[3:5]:
         load.wait()
     alpha = lx.rate / (1.0 + a_sub)
@@ -416,7 +423,6 @@
     mcat = jnp.concatenate([mh, mh, ml], axis=1)
 
     def rest():
-        lax.fori_loop(T2, LEV, toeplitz, 0)
         block()
 
     @pl.when(jnp.logical_not(middle))
@@ -424,6 +430,10 @@
         rest()
 
     done.append(chain(1))
+
+    @pl.when(centre)
+    def _():
+        spread()
 
     @pl.when(middle)
     def _():
@@ -440,10 +450,11 @@
         tt = pl.multiple_of(l * BY, BY)
         vh, vl = split(xr[pl.ds(l, 8, stride=LEV), :])
         th = thi[pl.ds(tt, BY), :]
-        xf[pl.ds(l, 8, stride=LEV), :] = dot(vh, th, NN) + dot(vl, th, NN) + dot(vh, tlo[pl.ds(tt, BY), :], NN)
-        return carry
-
-    lax.fori_loop(0, LEV, local_x, 0, unroll=4)
+        xf[pl.ds(l, 8, stride=LEV), :] = dot(jnp.concatenate([vh, vl, vh], axis=1),
+                                             jnp.concatenate([th, th, tlo[pl.ds(tt, BY), :]], axis=0), NN)
+        return carry
+
+    lax.fori_loop(0, LEV, local_x, 0, unroll=16)
     for cp in ccp:
         cp.wait()
     right = slot < 8
@@ -468,7 +479,7 @@
             xf[pl.ds(pl.multiple_of(j * LEV + t * 8, 8), 8), :] += res[j * 8:(j + 1) * 8]
         return carry
 
-    lax.fori_loop(0, LEV // 8, synth_x, 0)
+    lax.fori_loop(0, LEV // 8, synth_x, 0, unroll=8)
 
     g, s, e, G = lx.g, lx.s, lx.e, lx.G
     ge = 1.0 + g
@@ -510,10 +521,7 @@
             out[k, pl.ds(x, LEV, stride=BX), :] = dot(mcat, fcat, NN)
         return carry
 
-    lax.fori_loop(0, BX, mix, 0, unroll=2)
-    loads[5].wait()
-    for k in range(KLOC):
-        out[k] = out[k] + ctl_v[k].astype(F32)
+    lax.fori_loop(0, BX, mix, 0, unroll=8)
 
 
 def per_device(members, gradient, control, filter_rates, vertical_weights, band_widths):
@@ -528,7 +536,7 @@
     out = pl.pallas_call(
         kernel,
         out_shape=jax.ShapeDtypeStruct((KLOC, ROWS, BY), F32),
-        in_specs=[hbm] * 6,
+        in_specs=[hbm] * 5,
         out_specs=pl.BlockSpec(memory_space=pltpu.VMEM),
         scratch_shapes=[
             pltpu.SMEM((LEV,), F32),
@@ -536,7 +544,6 @@
             vm(LEV, LEV),
             pltpu.VMEM((KLOC, ROWS, BY), BF16),
             vm(ROWS, BY),
-            pltpu.VMEM((KLOC, ROWS, BY), BF16),
             vm(ROWS, BY), vm(ROWS, BY), vm(3, QUARTER, BY),
             vm(KLOC, ROWS, BY), vm(KLOC, ROWS, BY),
             vm(LEV * 8, 128), vm(LEV, 128),
@@ -552,7 +559,7 @@
             vm(GROUPS, 128), vm(GROUPS, 128), vm(GROUPS, 128), vm(7, GROUPS, 128),
             vm(8 * LEV, 128), vm(8 * LEV, 128),
             vm(KLOC, BX, LEV, BY),
-            dma((6,)),
+            dma((5,)),
             *three, *three, *three, *three, *three, *three,
             *single, *single,
             dma((2, CHUNKS)), dma((2, CHUNKS)), dma((2,)), dma((2,)),
@@ -563,9 +570,9 @@
         name="localize",
     )(
         filter_rates, band_widths.reshape(1, LEV), vertical_weights,
-        members.reshape(KLOC, ROWS, BY), gradient.reshape(ROWS, BY), control.reshape(KLOC, ROWS, BY),
+        members.reshape(KLOC, ROWS, BY), gradient.reshape(ROWS, BY),
     )
-    return out.reshape(KLOC, LEV, BX, BY)
+    return out.reshape(KLOC, LEV, BX, BY) + control.astype(F32)
 
 
 def solution(mesh):

time: 67.6 us -> 59.6 us (0.88)
  Pallas kernels: 65.1 us -> 57.2 us
  other arithmetic: 0 us -> 2.3 us
  local copies, waits for them, and re-layouts: 2.26 us -> 0.01 us
    pallas_call x1, Pallas kernels: 65.1 us -> 57.2 us  [per_device(): pl.pallas_call(kernel, out_shape=jax.ShapeDtypeStruct((KLOC, ROWS, BY), F...]
    add x0 -> x1, other arithmetic: none -> 2.3 us  [per_device(): return out.reshape(KLOC, LEV, BX, BY) + control.astype(F32)]
    unnamed x1 -> x2, local copies, waits for them, and re-layouts: 2.26 us -> 0.01 us
where the time goes in v2:
time: 59.6 us; the launch traced here: 59.5 us
  Pallas kernels  57.2 us (96%)
  other arithmetic  2.3 us (4%)
    pallas_call x1, Pallas kernels, per_device(): pl.pallas_call(kernel, out_shape=jax.ShapeDtypeStruct((KLOC, ROWS, BY), F...  57.2 us
    add x1, other arithmetic, per_device(): return out.reshape(KLOC, LEV, BX, BY) + control.astype(F32)  2.3 us

profile of v2, /device:TPU:1, one launch (start us, length us, event | category | flops | bytes accessed | tf_op | source)
XLA Modules:
  0.0 59.5 jit_solution(9359865074985195930)
XLA Ops:
  0.0 0.0 copy-start
  0.0 57.2 %localize.1 = f32[2,1024,128]{2,1,0:T(8,128)} custom-call(f32[64]{0:T(128)} %rates_h.1, s32[1,64]{1,0:T(1,128)} %bitcast.7, f32[64,64]{1,0:T(8,128)} %weights_h.1, bf16[2,1024,128]{2,1,0:T(8,128)(2,1)} %bitcast.5, f32[1024,128]{1,0:T(8,128)} %bitcast.6), custom_call_target="tpu_custom_call" | custom-call | tf_op jit(solution)/shard_map/localize/pallas_call | solution.py:536
  57.2 0.0 copy-done
  57.2 2.3 %convert_add_fusion = f32[2,64,16,128]{3,2,1,0:T(8,128)} fusion(f32[2,64,16,128]{3,2,1,0:T(8,128)} %bitcast.4, bf16[2,64,16,128]{3,2,1,0:T(8,128)(2,1)S(1)} %copy-done), kind=kLoop, calls=%fused_computation | loop fusion | flops 524288 | bytes 2621440 | tf_op jit(solution)/shard_map/add | solution.py:575
Async XLA Ops:
  0.0 57.2 %copy-start = (bf16[2,64,16,128]{3,2,1,0:T(8,128)(2,1)S(1)}, bf16[2,64,16,128]{3,2,1,0:T(8,128)(2,1)}, u32[]{:S(2)}) copy-start(bf16[2,64,16,128]{3,2,1,0:T(8,128)(2,1)} %param.8) | copy-start | bytes 1572868

commit v3 on v2

--- a/solution.py
+++ b/solution.py
@@ -20,6 +20,8 @@
 QUARTER = ROWS // MEM
 CHUNKS = 4
 CHUNK = LEV // CHUNKS
+PARTS = 2
+PART = LEV // PARTS
 
 NT = (((1,), (1,)), ((), ()))
 NN = (((1,), (0,)), ((), ()))
@@ -80,9 +82,9 @@
 
 def kernel(rates_h, bands_h, weights_h, members, gradient, out,
            rates, bands, weights, mem_v, grad_v, psum, total, rs_rcv, vbuf, zbuf, wtab, lsub, thi, tlo,
-           mu, ysum, yone, xsum, xrs, xmn, ysnd, yrcv, zsnd, zrcv, kap, xst, xpair, xin, xout, xss, xsr,
+           mu, ysum, yone, xsum, xrs, xmn, xrt, ysnd, yrcv, zsnd, zrcv, kap, xst, xpair, xin, xout, xss, xsr,
            cown, csib, ctot, crcv, xr, xf, fbuf,
-           in_sem, rs_s, rs_r, ag_s, ag_r, o_s, o_r, xs_s, xs_r, xa_s, xa_r, y_s, y_r, h_s, h_r, p_s, p_r,
+           in_sem, rs_s, rs_r, ag_s, ag_r, o_s, o_r, xs_s, xs_r, y_s, y_r, h_s, h_r, p_s, p_r,
            c_s, c_r, d_s, d_r, k_s, k_r, l_s, l_r):
     i = lax.axis_index("mem")
     gx = lax.axis_index("gx")
@@ -201,16 +203,20 @@
             xst[k, q] = s
             if k == 1:
                 xsum[q] = xst[0, q] + s
-    own16 = pl.multiple_of(i * 16, 16)
-    xrc = [remote(xsum.at[:, pl.ds(pl.multiple_of(peers[d][0] * 16, 16), 16)], xrs.at[d],
-                  xs_s.at[d], xs_r.at[d], peers[d]) for d in range(3)]
-    for cp in xrc:
-        cp.start()
-    rs = [remote(psum.at[pl.ds(pl.multiple_of(peers[d][0] * QUARTER, QUARTER), QUARTER)], rs_rcv.at[d],
-                 rs_s.at[d], rs_r.at[d], peers[d]) for d in range(3)]
-    for cp in rs:
-        cp.start()
-
+    ring = [(i + 1 - 2 * (i % 2), gx, gy), (3 - i, gx, gy)]
+
+    def piece(ref, half, c):
+        return ref.at[2 * half:2 * half + 2, c * PART:(c + 1) * PART]
+
+    def round_of(step, src, dst):
+        return [[remote(piece(src, half, c), piece(dst, half, c), xs_s.at[step, half, c], xs_r.at[step, half, c],
+                        ring[(half + step) % 2]) for half in range(2)] for c in range(PARTS)]
+
+    near = round_of(0, xsum, xrs)
+    far = round_of(1, xmn, xrt)
+    for pair in near:
+        for cp in pair:
+            cp.start()
     di = jnp.abs(iota((BY, BY), 0) - iota((BY, BY), 1)).astype(F32)
 
     def toeplitz(l, carry):
@@ -245,12 +251,16 @@
         cp.start()
         ycp.append(cp)
 
-    for cp in xrc:
-        cp.wait()
-    xmn[:, pl.ds(own16, 16)] = (xsum[:, pl.ds(own16, 16)] + xrs[0] + xrs[1] + xrs[2]) * (1.0 / MEMBERS)
-    xag = [remote(xmn.at[:, pl.ds(own16, 16)], xmn.at[:, pl.ds(own16, 16)], xa_s.at[d], xa_r.at[d], peers[d])
-           for d in range(3)]
-    for cp in xag:
+    for c in range(PARTS):
+        rows = slice(c * PART, (c + 1) * PART)
+        for cp in near[c]:
+            cp.wait()
+        xmn[:, rows] = xsum[:, rows] + xrs[:, rows]
+        for cp in far[c]:
+            cp.start()
+    rs = [remote(psum.at[pl.ds(pl.multiple_of(peers[d][0] * QUARTER, QUARTER), QUARTER)], rs_rcv.at[d],
+                 rs_s.at[d], rs_r.at[d], peers[d]) for d in range(3)]
+    for cp in rs:
         cp.start()
 
     for cp in ycp:
@@ -271,14 +281,19 @@
     hcp = remote(zsnd, zrcv, h_s, h_r, across)
     hcp.start()
 
-    for cp in xag:
-        cp.wait()
-    for k in range(KLOC):
-        xst[k] = xst[k] - xmn[...]
-    pcp = remote(xst.at[1 - core], xpair, p_s, p_r, sibling)
-    pcp.start()
-
-    pcp.wait()
+    pcp = []
+    for c in range(PARTS):
+        rows = slice(c * PART, (c + 1) * PART)
+        for cp in far[c]:
+            cp.wait()
+        for q in range(4):
+            m = (xmn[q, rows] + xrt[q, rows]) * (1.0 / MEMBERS)
+            for k in range(KLOC):
+                xst[k, q, rows] = xst[k, q, rows] - m
+        cp = remote(xst.at[1 - core, :, rows], xpair.at[:, rows], p_s.at[c], p_r.at[c], sibling)
+        cp.start()
+        pcp.append(cp)
+
 
     def chain(turn):
         way = ((z >= 4).astype(jnp.int32) + turn) % 2
@@ -297,6 +312,9 @@
 
         for c in range(CHUNKS):
             rows = slice(c * CHUNK, (c + 1) * CHUNK)
+
+            if turn == 0 and c % (CHUNKS // PARTS) == 0:
+                pcp[c // (CHUNKS // PARTS)].wait()
 
             @pl.when(has_in)
             def _():
@@ -356,6 +374,7 @@
     sh, sl = split(stack)
     res = dot(sh, seg, NN) + dot(sl, seg, NN)
     slot = lane % BX
+    slot8 = iota((8, 128), 1) % BX < 8
     cor = zero
     for c in range(16):
         cor = jnp.where(slot == c, res[c * GROUPS:(c + 1) * GROUPS], cor)
@@ -367,11 +386,15 @@
 
     def spread():
         lcp.wait()
-        ctot[...] = cor + csib[...]
+        even = cown[pl.ds(0, 8, stride=2), :] + csib[pl.ds(0, 8, stride=2), :]
+        odd = cown[pl.ds(1, 8, stride=2), :] + csib[pl.ds(1, 8, stride=2), :]
+        ctot[0] = jnp.where(slot8, even, pltpu.roll(odd, 8, 1))
+        ctot[1] = jnp.where(slot8, pltpu.roll(even, 120, 1), odd)
         for d in (3, 2, 4, 1, 5, 0, 6):
             ccp[d].start()
 
-    ccp = [remote(ctot, crcv.at[d], k_s.at[d], k_r.at[d], chips[d]) for d in range(7)]
+    to_right = [(z + d + 1) <= 7 for d in range(7)]
+    ccp = [remote(ctot.at[jnp.where(to_right[d], 0, 1)], crcv.at[d], k_s.at[d], k_r.at[d], chips[d]) for d in range(7)]
 
     def local_y(l, carry):
         at = pl.multiple_of(l * BX, BX)
@@ -404,7 +427,7 @@
         lax.fori_loop(0, LEV, local_y, 0, unroll=8)
         lax.fori_loop(0, GROUPS, synth, 0, unroll=4)
 
-    middle = (z >= 2) & (z <= 5)
+    middle = (z >= 1) & (z <= 6)
     centre = (z == 3) | (z == 4)
 
     @pl.when(jnp.logical_not(centre))
@@ -457,12 +480,15 @@
     lax.fori_loop(0, LEV, local_x, 0, unroll=16)
     for cp in ccp:
         cp.wait()
-    right = slot < 8
-    cst = jnp.where(right == (core == 1), csib[...], 0.0)
+    to_me, to_us = jnp.zeros((8, 128), F32), jnp.zeros((8, 128), F32)
     for d in range(7):
         from_left = (z - (d + 1)) >= 0
-        cst = cst + jnp.where(right == from_left, crcv[d], 0.0)
-    cown[...] = cst
+        to_me = to_me + jnp.where(from_left, crcv[d], 0.0)
+        to_us = to_us + jnp.where(from_left, 0.0, crcv[d])
+    mate = jnp.where((slot < 8) == (core == 1), csib[...], 0.0)
+    cown[...] = mate
+    cown[pl.ds(0, 8, stride=2), :] += jnp.where(slot8, to_me, pltpu.roll(to_us, 8, 1))
+    cown[pl.ds(1, 8, stride=2), :] += jnp.where(slot8, pltpu.roll(to_me, 120, 1), to_us)
     zr, zc = iota((64, 256), 0), iota((64, 256), 1)
     fits = ((zr // 32 == (zc // 64) % 2) & ((zr // 8) % 4 == (zc // 4) % 4)
             & ((zr % 8) // 4 == zc // 128) & (zr % 4 == (zc // 16) % 4))
@@ -535,7 +561,7 @@
     single = [dma] * 2
     out = pl.pallas_call(
         kernel,
-        out_shape=jax.ShapeDtypeStruct((KLOC, ROWS, BY), F32),
+        out_shape=pltpu.VMEM((KLOC, ROWS, BY), F32),
         in_specs=[hbm] * 5,
         out_specs=pl.BlockSpec(memory_space=pltpu.VMEM),
         scratch_shapes=[
@@ -551,27 +577,28 @@
             pltpu.VMEM((LEV * BY, BY), BF16),
             vm(GROUPS * 8, 128),
             vm(2, GROUPS, 128), vm(3, 2, GROUPS, 128),
-            vm(4, LEV, 128), vm(3, 4, 16, 128), vm(4, LEV, 128),
+            vm(4, LEV, 128), vm(4, LEV, 128), vm(4, LEV, 128), vm(4, LEV, 128),
             vm(4, GROUPS, 128), vm(3, 2, GROUPS, 128), vm(4, GROUPS, 128), vm(4, GROUPS, 128),
             vm(GROUPS * 8, 128),
             vm(KLOC, 4, LEV, 128), vm(4, LEV, 128),
             vm(2, 2, LEV, 128), vm(2, 2, LEV, 128), vm(2, 2, LEV, 128), vm(2, 2, LEV, 128),
-            vm(GROUPS, 128), vm(GROUPS, 128), vm(GROUPS, 128), vm(7, GROUPS, 128),
+            vm(GROUPS, 128), vm(GROUPS, 128), vm(2, 8, 128), vm(7, 8, 128),
             vm(8 * LEV, 128), vm(8 * LEV, 128),
             vm(KLOC, BX, LEV, BY),
             dma((5,)),
-            *three, *three, *three, *three, *three, *three,
-            *single, *single,
+            *three, *three, *three, dma((2, 2, PARTS)), dma((2, 2, PARTS)), *three,
+            *single, dma((PARTS,)), dma((PARTS,)),
             dma((2, CHUNKS)), dma((2, CHUNKS)), dma((2,)), dma((2,)),
             dma((7,)), dma((7,)), *single,
         ],
         compiler_params=pltpu.CompilerParams(
-            collective_id=0, has_side_effects=True, vmem_limit_bytes=60 << 20),
+            collective_id=0, has_side_effects=True, vmem_limit_bytes=48 << 20),
         name="localize",
-    )(
-        filter_rates, band_widths.reshape(1, LEV), vertical_weights,
-        members.reshape(KLOC, ROWS, BY), gradient.reshape(ROWS, BY),
-    )
+    )(*[
+        pltpu.with_memory_space_constraint(v, pltpu.HBM)
+        for v in (filter_rates, band_widths.reshape(1, LEV), vertical_weights,
+                  members.reshape(KLOC, ROWS, BY), gradient.reshape(ROWS, BY))
+    ])
     return out.reshape(KLOC, LEV, BX, BY) + control.astype(F32)
 
 

time: 59.6 us -> 54.5 us (0.914)
  Pallas kernels: 57.2 us -> 53.2 us
  other arithmetic: 2.3 us -> 1.07 us
    pallas_call x1, Pallas kernels: 57.2 us -> 53.2 us  [per_device(): pl.pallas_call(kernel, out_shape=pltpu.VMEM((KLOC, ROWS, BY), F32), in_sp...]
    add x1, other arithmetic: 2.3 us -> 1.07 us  [per_device(): return out.reshape(KLOC, LEV, BX, BY) + control.astype(F32)]
where the time goes in v3:
time: 54.5 us; the launch traced here: 54.3 us
  Pallas kernels  53.2 us (98%)
  other arithmetic  1.07 us (2%)
    pallas_call x1, Pallas kernels, per_device(): pl.pallas_call(kernel, out_shape=pltpu.VMEM((KLOC, ROWS, BY), F32), in_sp...  53.2 us

profile of v3, /device:TPU:1, one launch (start us, length us, event | category | flops | bytes accessed | tf_op | source)
XLA Modules:
  0.0 54.3 jit_solution(422849975824094953)
XLA Ops:
  0.0 0.0 copy-start
  0.0 53.2 %localize.1 = f32[2,1024,128]{2,1,0:T(8,128)S(1)} custom-call(f32[64]{0:T(128)} %rates_h.1, s32[1,64]{1,0:T(1,128)} %bitcast.7, f32[64,64]{1,0:T(8,128)} %weights_h.1, bf16[2,1024,128]{2,1,0:T(8,128)(2,1)} %bitcast.5, f32[1024,128]{1,0:T(8,128)} %bitcast.6), custom_call_target="tpu_custom_call" | custom-call | tf_op jit(solution)/shard_map/localize/pallas_call | solution.py:562
  53.3 0.0 copy-done
  53.3 1.1 %convert_add_fusion = f32[2,64,16,128]{3,2,1,0:T(8,128)} fusion(f32[2,64,16,128]{3,2,1,0:T(8,128)S(1)} %bitcast.4, bf16[2,64,16,128]{3,2,1,0:T(8,128)(2,1)S(1)} %copy-done), kind=kLoop, calls=%fused_computation | loop fusion | flops 524288 | bytes 2621440 | tf_op jit(solution)/shard_map/add | solution.py:602
Async XLA Ops:
  0.0 53.3 %copy-start = (bf16[2,64,16,128]{3,2,1,0:T(8,128)(2,1)S(1)}, bf16[2,64,16,128]{3,2,1,0:T(8,128)(2,1)}, u32[]{:S(2)}) copy-start(bf16[2,64,16,128]{3,2,1,0:T(8,128)(2,1)} %param.8) | copy-start | bytes 1572868

commit v4 on v3

--- a/solution.py
+++ b/solution.py
@@ -182,11 +182,6 @@
     ysum[0] = jnp.where(low, two[0], two[1])
     ysum[1] = jnp.where(low, two[2], two[3])
 
-    pl.semaphore_wait(barrier, 15)
-    one = [remote(ysum, yone.at[d], o_s.at[d], o_r.at[d], peers[d]) for d in range(3)]
-    for cp in one:
-        cp.start()
-
     for k in range(KLOC):
         r1 = jnp.zeros((LEV, 128), F32)
         r2, q1, q2 = r1, r1, r1
@@ -203,6 +198,11 @@
             xst[k, q] = s
             if k == 1:
                 xsum[q] = xst[0, q] + s
+    pl.semaphore_wait(barrier, 15)
+    one = [remote(ysum, yone.at[d], o_s.at[d], o_r.at[d], peers[d]) for d in range(3)]
+    for cp in one:
+        cp.start()
+
     ring = [(i + 1 - 2 * (i % 2), gx, gy), (3 - i, gx, gy)]
 
     def piece(ref, half, c):

time: 54.5 us -> 54.4 us (level)
  no operation moved by 1% of the time
where the time goes in v4:
time: 54.4 us; the launch traced here: 54.2 us
  Pallas kernels  53.2 us (98%)
  other arithmetic  1.07 us (2%)
    pallas_call x1, Pallas kernels, per_device(): pl.pallas_call(kernel, out_shape=pltpu.VMEM((KLOC, ROWS, BY), F32), in_sp...  53.2 us

profile of v4, /device:TPU:1, one launch (start us, length us, event | category | flops | bytes accessed | tf_op | source)
XLA Modules:
  0.0 54.2 jit_solution(2759131132817689795)
XLA Ops:
  0.0 0.0 copy-start
  0.0 53.2 %localize.1 = f32[2,1024,128]{2,1,0:T(8,128)S(1)} custom-call(f32[64]{0:T(128)} %rates_h.1, s32[1,64]{1,0:T(1,128)} %bitcast.7, f32[64,64]{1,0:T(8,128)} %weights_h.1, bf16[2,1024,128]{2,1,0:T(8,128)(2,1)} %bitcast.5, f32[1024,128]{1,0:T(8,128)} %bitcast.6), custom_call_target="tpu_custom_call" | custom-call | tf_op jit(solution)/shard_map/localize/pallas_call | solution.py:562
  53.2 0.0 copy-done
  53.2 1.1 %convert_add_fusion = f32[2,64,16,128]{3,2,1,0:T(8,128)} fusion(f32[2,64,16,128]{3,2,1,0:T(8,128)S(1)} %bitcast.4, bf16[2,64,16,128]{3,2,1,0:T(8,128)(2,1)S(1)} %copy-done), kind=kLoop, calls=%fused_computation | loop fusion | flops 524288 | bytes 2621440 | tf_op jit(solution)/shard_map/add | solution.py:602
Async XLA Ops:
  0.0 53.2 %copy-start = (bf16[2,64,16,128]{3,2,1,0:T(8,128)(2,1)S(1)}, bf16[2,64,16,128]{3,2,1,0:T(8,128)(2,1)}, u32[]{:S(2)}) copy-start(bf16[2,64,16,128]{3,2,1,0:T(8,128)(2,1)} %param.8) | copy-start | bytes 1572868

commit v5 on v4

--- a/solution.py
+++ b/solution.py
@@ -18,8 +18,6 @@
 ROWS = LEV * BX
 GROUPS = LEV // 4
 QUARTER = ROWS // MEM
-CHUNKS = 4
-CHUNK = LEV // CHUNKS
 PARTS = 2
 PART = LEV // PARTS
 
@@ -82,7 +80,7 @@
 
 def kernel(rates_h, bands_h, weights_h, members, gradient, out,
            rates, bands, weights, mem_v, grad_v, psum, total, rs_rcv, vbuf, zbuf, wtab, lsub, thi, tlo,
-           mu, ysum, yone, xsum, xrs, xmn, xrt, ysnd, yrcv, zsnd, zrcv, kap, xst, xpair, xin, xout, xss, xsr,
+           mu, ysum, yone, xsum, xrs, xmn, xrt, ysnd, yrcv, zsnd, zrcv, kap, xst, xpair, xin, xout, xlo, xss, xsr,
            cown, csib, ctot, crcv, xr, xf, fbuf,
            in_sem, rs_s, rs_r, ag_s, ag_r, o_s, o_r, xs_s, xs_r, y_s, y_r, h_s, h_r, p_s, p_r,
            c_s, c_r, d_s, d_r, k_s, k_r, l_s, l_r):
@@ -295,53 +293,69 @@
         pcp.append(cp)
 
 
-    def chain(turn):
-        way = ((z >= 4).astype(jnp.int32) + turn) % 2
-        has_in = jnp.where(way == 0, z > 0, z < 7)
-        has_out = jnp.where(way == 0, z < 7, z > 0)
-        target = (i, gx + 2 - 4 * way, gy)
-        part = pl.multiple_of(way * 2, 2)
-
-        def copy(c):
-            rows = pl.ds(c * CHUNK, CHUNK)
-            return remote(xout.at[way, :, rows], xin.at[way, :, rows], c_s.at[way, c], c_r.at[way, c], target)
-
-        @pl.when(jnp.logical_not(has_in))
-        def _():
-            xin[way] = jnp.zeros((2, LEV, 128), F32)
-
-        for c in range(CHUNKS):
-            rows = slice(c * CHUNK, (c + 1) * CHUNK)
-
-            if turn == 0 and c % (CHUNKS // PARTS) == 0:
-                pcp[c // (CHUNKS // PARTS)].wait()
-
-            @pl.when(has_in)
+    def comes(r, way):
+        return z >= (1 << r) if way == 0 else z + (1 << r) <= 7
+
+    def leaves(r, way):
+        return z + (1 << r) <= 7 if way == 0 else z >= (1 << r)
+
+    def hop(r, way, c):
+        rows = pl.ds(c * PART, PART)
+        step = (2 << r) * (1 - 2 * way)
+        return remote(xout.at[r, way, :, rows], xin.at[r, way, :, rows], c_s.at[r, way, c], c_r.at[r, way, c],
+                      (i, gx + step, gy))
+
+    for r in range(3):
+        for way in range(2):
+            @pl.when(jnp.logical_not(comes(r, way)))
             def _():
-                copy(c).wait_recv()
-
-            @pl.when(has_out)
-            def _():
-                xout[way, :, rows] = (xin[way, :, rows] + xst[core, pl.ds(part, 2), rows]
-                                      + xpair[pl.ds(part, 2), rows])
-                copy(c).start()
-
-        add = jnp.where(way == core, 1.0, 0.0)
-        xss[way] = xin[way] + add * xst[core, pl.ds(part, 2)]
-        sib = remote(xss.at[way], xsr.at[way], d_s.at[way], d_r.at[way], sibling)
-        sib.start()
-        xin[way] = xin[way] + (1.0 - add) * xpair[pl.ds(part, 2)]
-        return way, has_out, copy, sib
-
-    def drain(done):
-        for way, has_out, copy, sib in done:
+                xin[r, way] = jnp.zeros((2, LEV, 128), F32)
+
+    def rounds(r):
+        for c in range(PARTS):
+            rows = slice(c * PART, (c + 1) * PART)
+            if r == 0:
+                pcp[c].wait()
+            for way in range(2):
+                if r == 0:
+                    xout[0, way, :, rows] = xst[core, 2 * way:2 * way + 2, rows] + xpair[2 * way:2 * way + 2, rows]
+                else:
+                    @pl.when(comes(r - 1, way))
+                    def _():
+                        hop(r - 1, way, c).wait_recv()
+
+                    xout[r, way, :, rows] = xout[r - 1, way, :, rows] + xin[r - 1, way, :, rows]
+
+                @pl.when(leaves(r, way))
+                def _():
+                    hop(r, way, c).start()
+
+    def collect():
+        sibs = []
+        for way in range(2):
+            for c in range(PARTS):
+                @pl.when(comes(2, way))
+                def _():
+                    hop(2, way, c).wait_recv()
+
+            before = xin[0, way] + xin[1, way] + xin[2, way]
+            add = jnp.where(way == core, 1.0, 0.0)
+            xss[way] = before + add * xst[core, 2 * way:2 * way + 2]
+            sib = remote(xss.at[way], xsr.at[way], d_s.at[way], d_r.at[way], sibling)
+            sib.start()
+            sibs.append(sib)
+            xlo[way] = before + (1.0 - add) * xpair[2 * way:2 * way + 2]
+        for sib in sibs:
             sib.wait()
-            for c in range(CHUNKS):
-                @pl.when(has_out)
-                def _():
-                    copy(c).wait_send()
-
-    done = [chain(0)]
+        for r in range(3):
+            for way in range(2):
+                for c in range(PARTS):
+                    @pl.when(leaves(r, way))
+                    def _():
+                        hop(r, way, c).wait_send()
+
+    rounds(0)
+    rounds(1)
     own = pl.multiple_of(i * QUARTER, QUARTER)
     for cp in rs:
         cp.wait()
@@ -427,13 +441,9 @@
         lax.fori_loop(0, LEV, local_y, 0, unroll=8)
         lax.fori_loop(0, GROUPS, synth, 0, unroll=4)
 
-    middle = (z >= 1) & (z <= 6)
-    centre = (z == 3) | (z == 4)
-
-    @pl.when(jnp.logical_not(centre))
-    def _():
-        spread()
-
+
+    rounds(2)
+    spread()
     for load in loads[3:5]:
         load.wait()
     alpha = lx.rate / (1.0 + a_sub)
@@ -448,26 +458,13 @@
     def rest():
         block()
 
-    @pl.when(jnp.logical_not(middle))
-    def _():
-        rest()
-
-    done.append(chain(1))
-
-    @pl.when(centre)
-    def _():
-        spread()
-
-    @pl.when(middle)
-    def _():
-        rest()
-
-    drain(done)
+    rest()
+    collect()
 
     for k in range(KLOC):
         for q in range(4):
             row = (k * 4 + q) * LEV
-            xr[row:row + LEV, :] = jnp.where(core == k, xin[q // 2, q % 2], xsr[q // 2, q % 2])
+            xr[row:row + LEV, :] = jnp.where(core == k, xlo[q // 2, q % 2], xsr[q // 2, q % 2])
 
     def local_x(l, carry):
         tt = pl.multiple_of(l * BY, BY)
@@ -581,14 +578,14 @@
             vm(4, GROUPS, 128), vm(3, 2, GROUPS, 128), vm(4, GROUPS, 128), vm(4, GROUPS, 128),
             vm(GROUPS * 8, 128),
             vm(KLOC, 4, LEV, 128), vm(4, LEV, 128),
-            vm(2, 2, LEV, 128), vm(2, 2, LEV, 128), vm(2, 2, LEV, 128), vm(2, 2, LEV, 128),
+            vm(3, 2, 2, LEV, 128), vm(3, 2, 2, LEV, 128), vm(2, 2, LEV, 128), vm(2, 2, LEV, 128), vm(2, 2, LEV, 128),
             vm(GROUPS, 128), vm(GROUPS, 128), vm(2, 8, 128), vm(7, 8, 128),
             vm(8 * LEV, 128), vm(8 * LEV, 128),
             vm(KLOC, BX, LEV, BY),
             dma((5,)),
             *three, *three, *three, dma((2, 2, PARTS)), dma((2, 2, PARTS)), *three,
             *single, dma((PARTS,)), dma((PARTS,)),
-            dma((2, CHUNKS)), dma((2, CHUNKS)), dma((2,)), dma((2,)),
+            dma((3, 2, PARTS)), dma((3, 2, PARTS)), dma((2,)), dma((2,)),
             dma((7,)), dma((7,)), *single,
         ],
         compiler_params=pltpu.CompilerParams(

time: 54.4 us -> 52.3 us (0.961)
  Pallas kernels: 53.2 us -> 51.1 us
    pallas_call x1, Pallas kernels: 53.2 us -> 51.1 us  [per_device(): pl.pallas_call(kernel, out_shape=pltpu.VMEM((KLOC, ROWS, BY), F32), in_sp...]
where the time goes in v5:
time: 52.3 us; the launch traced here: 52.2 us
  Pallas kernels  51.1 us (98%)
  other arithmetic  1.07 us (2%)
    pallas_call x1, Pallas kernels, per_device(): pl.pallas_call(kernel, out_shape=pltpu.VMEM((KLOC, ROWS, BY), F32), in_sp...  51.1 us
    add x1, other arithmetic, per_device(): return out.reshape(KLOC, LEV, BX, BY) + control.astype(F32)  1.07 us

profile of v5, /device:TPU:1, one launch (start us, length us, event | category | flops | bytes accessed | tf_op | source)
XLA Modules:
  0.0 52.2 jit_solution(3909984418131088140)
XLA Ops:
  0.0 0.0 copy-start
  0.0 51.1 %localize.1 = f32[2,1024,128]{2,1,0:T(8,128)S(1)} custom-call(f32[64]{0:T(128)} %rates_h.1, s32[1,64]{1,0:T(1,128)} %bitcast.7, f32[64,64]{1,0:T(8,128)} %weights_h.1, bf16[2,1024,128]{2,1,0:T(8,128)(2,1)} %bitcast.5, f32[1024,128]{1,0:T(8,128)} %bitcast.6), custom_call_target="tpu_custom_call" | custom-call | tf_op jit(solution)/shard_map/localize/pallas_call | solution.py:559
  51.1 0.0 copy-done
  51.1 1.1 %convert_add_fusion = f32[2,64,16,128]{3,2,1,0:T(8,128)} fusion(f32[2,64,16,128]{3,2,1,0:T(8,128)S(1)} %bitcast.4, bf16[2,64,16,128]{3,2,1,0:T(8,128)(2,1)S(1)} %copy-done), kind=kLoop, calls=%fused_computation | loop fusion | flops 524288 | bytes 2621440 | tf_op jit(solution)/shard_map/add | solution.py:599
Async XLA Ops:
  0.0 51.1 %copy-start = (bf16[2,64,16,128]{3,2,1,0:T(8,128)(2,1)S(1)}, bf16[2,64,16,128]{3,2,1,0:T(8,128)(2,1)}, u32[]{:S(2)}) copy-start(bf16[2,64,16,128]{3,2,1,0:T(8,128)(2,1)} %param.8) | copy-start | bytes 1572868
